TPU v7x, 32 devices: a whole 2x2x4 slice. The times are simulated.
32 devices in a mesh: dp: 8 (over y, x, core), tensor: 4 (over z).
Axes of the slice: x: 2, y: 2, z: 4, core: 2. Of those that a mesh axis runs over, the one named last changes fastest.
Arguments:
- block_input: bfloat16 [16384, 1536], P('dp'), may hold values from -6 to 6
- segment_ids: int32 [16384], P('dp'), may hold values from 0 to 16383, as said below
- norm_gain: float32 [1536], replicated, may hold values from 0.1 to 1.9
- gate_weight: bfloat16 [1536, 3072], P(None, 'tensor'), may hold values from -0.15625 to 0.15625
- input_weight: bfloat16 [1536, 3072], P(None, 'tensor'), may hold values from -0.15625 to 0.15625
- state_weight: bfloat16 [1536, 256], replicated, may hold values from -0.15625 to 0.15625
- step_weight: bfloat16 [1536, 48], P(None, 'tensor'), may hold values from -0.15625 to 0.15625
- mixer_conv: float32 [4, 3072], P(None, 'tensor'), may hold values from -3 to 3
- mixer_shift: float32 [3072], P('tensor'), may hold values from -3 to 3
- state_conv: float32 [4, 256], replicated, may hold values from -3 to 3
- state_shift: float32 [256], replicated, may hold values from -3 to 3
- step_bias: float32 [48], P('tensor'), may hold values from -6.9 to -2.3
- decay_log: float32 [48], P('tensor'), may hold values from 0 to 2.77
- skip_gain: float32 [48], P('tensor'), may hold values from -4 to 4
- gate_gain: float32 [3072], P('tensor'), may hold values from 0.1 to 1.9
- out_weight: bfloat16 [3072, 1536], P('tensor'), may hold values from -0.109375 to 0.109375
- out_grad: bfloat16 [16384, 1536], P('dp'), may hold values from -6 to 6
Outputs:
- block_output: bfloat16 [16384, 1536], P('dp')
- input_grad: bfloat16 [16384, 1536], P('dp')
- norm_gain_grad: float32 [1536], P('tensor')
- gate_weight_grad: float32 [1536, 3072], P(None, 'tensor')
- input_weight_grad: float32 [1536, 3072], P(None, 'tensor')
- state_weight_grad: float32 [1536, 256], P('tensor')
- step_weight_grad: float32 [1536, 48], P(None, 'tensor')
- mixer_conv_grad: float32 [4, 3072], P(None, 'tensor')
- mixer_shift_grad: float32 [3072], P('tensor')
- state_conv_grad: float32 [4, 256], replicated
- state_shift_grad: float32 [256], replicated
- step_bias_grad: float32 [48], P('tensor')
- decay_log_grad: float32 [48], P('tensor')
- skip_gain_grad: float32 [48], P('tensor')
- gate_gain_grad: float32 [3072], P('tensor')
- out_weight_grad: float32 [3072, 1536], P('tensor')
Inputs may be any that keep to these rules, and one draw needn't show every extreme that they name: `segment_ids`: each token's number is the position, in the whole array, of the first token of its document; documents are 200 to 2000 tokens long unless cut at the end of a packed sequence of 2048 tokens, and none crosses such an end.
All inputs are finite; a program needn't handle non-finite values.
Results may differ from a plain program's by a relative error of at most 0.024.
Values may be sent and summed in bfloat16 or wider, within the bound.
No kernel may reach another device: no remote copies, remote signals or barrier semaphores. Data moves between devices by JAX's collectives and lax.ppermute only.
A program may use at most 256 MiB of HBM per device.

v0:
```python
import jax
import jax.numpy as jnp
from jax import lax
from jax.sharding import PartitionSpec as P

epsilon = 1e-05
highest = lax.Precision.HIGHEST


def product(left, right):
    return jnp.dot(left, right, precision=highest, preferred_element_type=jnp.float32)


def fast(left, right):
    return jnp.dot(left, right, preferred_element_type=jnp.float32)


def contract_rows(left, right):
    return lax.dot_general(
        left, right, (((0,), (0,)), ((), ())), preferred_element_type=jnp.float32
    )


def against_rows(left, right):
    return lax.dot_general(
        left, right, (((1,), (1,)), ((), ())), preferred_element_type=jnp.float32
    )


def silu_slope(values):
    sigma = jax.nn.sigmoid(values)
    return sigma * (1.0 + values * (1.0 - sigma))


def shift_rows(values, offset):
    return jnp.pad(values, ((offset, 0), (0, 0)))[: values.shape[0]]


def shift_segments(segments, offset):
    filler = jnp.full((offset,), -1, jnp.int32)
    return jnp.concatenate([filler, segments[: segments.shape[0] - offset]])


def causal_conv(values, weight, shift, segments):
    total = shift[None, :] + weight[0][None, :] * values
    for offset in range(1, weight.shape[0]):
        same = (shift_segments(segments, offset) == segments).astype(values.dtype)
        total = total + weight[offset][None, :] * shift_rows(values, offset) * same[:, None]
    return total


def on_device(
    block_input,
    segment_ids,
    norm_gain,
    gate_weight,
    input_weight,
    state_weight,
    step_weight,
    mixer_conv,
    mixer_shift,
    state_conv,
    state_shift,
    step_bias,
    decay_log,
    skip_gain,
    gate_gain,
    out_weight,
    out_grad,
):
    length, width = block_input.shape
    inner_local = gate_weight.shape[1]
    groups = lax.axis_size("tensor")
    member = lax.axis_index("tensor")
    share = length // groups
    columns = width // groups
    row_start = member * share
    column_start = member * columns
    half = state_weight.shape[1] // 2
    inner_total = inner_local * groups
    residual = block_input.astype(jnp.float32)
    inverse_rms = lax.rsqrt(jnp.mean(residual * residual, axis=-1, keepdims=True) + epsilon)
    unit_rows = residual * inverse_rms
    normed = (unit_rows * norm_gain).astype(jnp.bfloat16)
    gate_raw = fast(normed, gate_weight).astype(jnp.bfloat16)
    mixer_raw = fast(normed, input_weight).astype(jnp.bfloat16)
    state_raw = fast(normed, state_weight).astype(jnp.bfloat16)
    step_raw = fast(normed, step_weight).astype(jnp.bfloat16)

    def conv_active(values, weight, shift):
        return jax.nn.silu(causal_conv(values, weight, shift, segment_ids))

    mixer_act, mixer_pull = jax.vjp(
        conv_active, mixer_raw.astype(jnp.float32), mixer_conv, mixer_shift
    )
    mixer_in = mixer_act.astype(jnp.bfloat16)
    state_act, state_pull = jax.vjp(
        conv_active, state_raw.astype(jnp.float32), state_conv, state_shift
    )
    states = state_act.astype(jnp.bfloat16)
    state_b = states[:, :half]
    state_c = states[:, half:]
    step_field = step_raw.astype(jnp.float32) + step_bias
    step_size = jax.nn.softplus(step_field)
    heads_local = step_size.shape[1]
    scores = against_rows(state_c, state_b)
    place = jnp.arange(length)
    mask = (
        (place[:, None] >= place[None, :]) & (segment_ids[:, None] == segment_ids[None, :])
    ).astype(jnp.float32)
    rates = -jnp.exp(decay_log)
    levels = jnp.cumsum(step_size * rates[None, :], axis=0)
    head_values = jnp.moveaxis(mixer_in.reshape(length, heads_local, -1), 1, 0)
    values_float = mixer_in.astype(jnp.float32).reshape(length, heads_local, -1)

    def head_weights(head_step, head_level):
        spread = jnp.where(mask > 0, head_level[:, None] - head_level[None, :], 0.0)
        damping = jnp.exp(spread) * mask
        return (scores * damping * head_step[None, :], damping)

    def forward_head(item):
        values_head, step_head, level_head = item
        weights, damping = head_weights(step_head, level_head)
        return fast(weights.astype(jnp.bfloat16), values_head)

    mixed_heads = lax.map(forward_head, (head_values, step_size.T, levels.T))
    mixed = (jnp.moveaxis(mixed_heads, 0, 1) + skip_gain[None, :, None] * values_float).reshape(
        length, -1
    )
    gate_field = gate_raw.astype(jnp.float32)
    gate_act = jax.nn.silu(gate_field)
    gated = mixed * gate_act
    square_sums = lax.psum(jnp.sum(gated * gated, axis=-1), "tensor")
    gate_rms = lax.rsqrt(square_sums[:, None] / inner_total + epsilon)
    gate_unit = gated * gate_rms
    gate_out = (gate_unit * gate_gain).astype(jnp.bfloat16)
    summed = lax.psum(fast(gate_out, out_weight), "tensor")
    block_output = (summed + residual).astype(jnp.bfloat16)
    gate_out_grad = against_rows(out_grad, out_weight)
    out_weight_grad = contract_rows(gate_out, out_grad)
    gate_gain_grad = jnp.sum(gate_out_grad * gate_unit, axis=0)
    unit_grad = gate_out_grad * gate_gain
    cross = lax.psum(jnp.sum(unit_grad * gated, axis=-1), "tensor")
    gated_grad = gate_rms * unit_grad - gate_rms * gate_rms * gate_rms * gated * (
        cross[:, None] / inner_total
    )
    mixed_grad = gated_grad * gate_act
    mixed_low = mixed_grad.astype(jnp.bfloat16)
    gate_raw_grad = (gated_grad * mixed * silu_slope(gate_field)).astype(jnp.bfloat16)
    head_cotangents = jnp.moveaxis(mixed_low.reshape(length, heads_local, -1), 1, 0)

    def backward_head(score_grad, item):
        values_head, cotangent_head, step_head, level_head = item
        weights, damping = head_weights(step_head, level_head)
        cell_grad = against_rows(cotangent_head, values_head) * mask
        values_grad = contract_rows(weights.astype(jnp.bfloat16), cotangent_head)
        scaled = cell_grad * damping
        touched = scaled * scores
        column_sums = jnp.sum(touched, axis=0)
        level_grad = jnp.sum(touched * step_head[None, :], axis=1) - column_sums * step_head
        return (score_grad + scaled * step_head[None, :], (values_grad, level_grad, column_sums))

    score_grad, (values_grads, level_grads, column_grads) = lax.scan(
        backward_head,
        jnp.zeros((length, length), jnp.float32),
        (head_values, head_cotangents, step_size.T, levels.T),
    )
    reach = jnp.flip(jnp.cumsum(jnp.flip(level_grads, 1), axis=1), 1).T
    step_size_grad = column_grads.T + reach * rates[None, :]
    decay_log_grad = jnp.sum(reach * step_size, axis=0) * rates
    low_float = mixed_low.astype(jnp.float32).reshape(length, heads_local, -1)
    skip_gain_grad = jnp.sum(low_float * values_float, axis=(0, 2))
    mixer_in_grad = (
        jnp.moveaxis(values_grads, 0, 1) + skip_gain[None, :, None] * low_float
    ).reshape(length, -1)
    state_c_grad = product(score_grad, state_b.astype(jnp.float32))
    state_b_grad = lax.dot_general(
        score_grad,
        state_c.astype(jnp.float32),
        (((0,), (0,)), ((), ())),
        precision=highest,
        preferred_element_type=jnp.float32,
    )
    states_grad = lax.psum(jnp.concatenate([state_b_grad, state_c_grad], axis=1), "tensor")
    mixer_raw_grad, mixer_conv_grad, mixer_shift_grad = mixer_pull(mixer_in_grad)
    state_raw_grad, state_conv_grad, state_shift_grad = state_pull(states_grad)
    step_field_grad = step_size_grad * jax.nn.sigmoid(step_field)
    step_bias_grad = jnp.sum(step_field_grad, axis=0)
    mixer_raw_low = mixer_raw_grad.astype(jnp.bfloat16)
    state_raw_low = state_raw_grad.astype(jnp.bfloat16)
    step_raw_low = step_field_grad.astype(jnp.bfloat16)
    gate_weight_grad = contract_rows(normed, gate_raw_grad)
    input_weight_grad = contract_rows(normed, mixer_raw_low)
    step_weight_grad = contract_rows(normed, step_raw_low)
    own_columns = lax.dynamic_slice_in_dim(normed, column_start, columns, 1)
    state_weight_grad = contract_rows(own_columns, state_raw_low)
    normed_partial = (
        against_rows(gate_raw_grad, gate_weight)
        + against_rows(mixer_raw_low, input_weight)
        + against_rows(step_raw_low, step_weight)
    )
    own_state = against_rows(
        lax.dynamic_slice_in_dim(state_raw_low, row_start, share, 0), state_weight
    )
    normed_partial = lax.dynamic_update_slice_in_dim(
        normed_partial,
        lax.dynamic_slice_in_dim(normed_partial, row_start, share, 0) + own_state,
        row_start,
        0,
    )
    normed_grad = lax.psum(normed_partial, "tensor")
    norm_gain_grad = jnp.sum(
        lax.dynamic_slice_in_dim(normed_grad, column_start, columns, 1)
        * lax.dynamic_slice_in_dim(unit_rows, column_start, columns, 1),
        axis=0,
    )
    unit_back = normed_grad * norm_gain
    full_grad = inverse_rms * (
        unit_back - unit_rows * jnp.mean(unit_back * unit_rows, axis=-1, keepdims=True)
    )
    input_grad = (full_grad + out_grad.astype(jnp.float32)).astype(jnp.bfloat16)
    (
        norm_gain_grad,
        gate_weight_grad,
        input_weight_grad,
        state_weight_grad,
        step_weight_grad,
        mixer_conv_grad,
        mixer_shift_grad,
        state_conv_grad,
        state_shift_grad,
        step_bias_grad,
        decay_log_grad,
        skip_gain_grad,
        gate_gain_grad,
        out_weight_grad,
    ) = lax.psum(
        (
            norm_gain_grad,
            gate_weight_grad,
            input_weight_grad,
            state_weight_grad,
            step_weight_grad,
            mixer_conv_grad,
            mixer_shift_grad,
            state_conv_grad,
            state_shift_grad,
            step_bias_grad,
            decay_log_grad,
            skip_gain_grad,
            gate_gain_grad,
            out_weight_grad,
        ),
        "dp",
    )
    return (
        block_output,
        input_grad,
        norm_gain_grad,
        gate_weight_grad,
        input_weight_grad,
        state_weight_grad,
        step_weight_grad,
        mixer_conv_grad,
        mixer_shift_grad,
        state_conv_grad,
        state_shift_grad,
        step_bias_grad,
        decay_log_grad,
        skip_gain_grad,
        gate_gain_grad,
        out_weight_grad,
    )


def solution(mesh):
    return jax.shard_map(
        on_device,
        mesh=mesh,
        in_specs=(
            P("dp", None),
            P("dp"),
            P(),
            P(None, "tensor"),
            P(None, "tensor"),
            P(),
            P(None, "tensor"),
            P(None, "tensor"),
            P("tensor"),
            P(),
            P(),
            P("tensor"),
            P("tensor"),
            P("tensor"),
            P("tensor"),
            P("tensor", None),
            P("dp", None),
        ),
        out_specs=(
            P("dp", None),
            P("dp", None),
            P("tensor"),
            P(None, "tensor"),
            P(None, "tensor"),
            P("tensor", None),
            P(None, "tensor"),
            P(None, "tensor"),
            P("tensor"),
            P(),
            P(),
            P("tensor"),
            P("tensor"),
            P("tensor"),
            P("tensor"),
            P("tensor", None),
        ),
        check_vma=False,
    )
```

profile of v0, /device:TPU:0, one launch (start us, length us, event | category | flops | bytes accessed | tf_op | source)
XLA Modules:
  0.0 1951.3 jit_solution(10041615015695338113)
XLA Ops:
  11.6 11.1 convert_multiply_fusion
  22.8 8.1 fusion.50
  31.1 7.5 multiply_convert_fusion.9
  64.4 8.1 fusion.65
  82.5 147.0 %while.30 = (s32[]{:T(128)}, f32[12,2048,64]{1,2,0:T(8,128)}, f32[12,2048]{1,0:T(8,128)S(1)}, f32[2048,2048]{1,0:T(8,128)}, f32[12,2048]{1,0:T(8,128)S(1)}, /*index=5*/bf16[12,2048,64]{2,1,0:T(8,128)(2,1)}, s32[2048]{0:T(1024)S(1)}) while((s32[]{:T(128)}, f32[12,2048,64]{1,2,0:T(8,128)}, f32[12,2048]{1,0:T(8,128)S(1)}, ...), condition=%wide.region_4.5_spmd.clone.clone, body=%wide.region_3.4_spmd.clone.sunk.clone | while | flops 583008256 | bytes 17900624 | solution.py:126
  83.1 12.2 fusion.141
  95.3 12.2 fusion.141
  107.5 12.2 fusion.141
  119.7 12.2 fusion.141
  131.9 12.2 fusion.141
  144.1 12.2 fusion.141
  156.3 12.2 fusion.141
  168.5 12.2 fusion.141
  180.7 12.2 fusion.141
  192.9 12.2 fusion.141
  205.1 12.2 fusion.141
  217.3 12.2 fusion.141
  229.5 9.5 bitcast_add_fusion.1
  245.6 10.7 multiply_reduce_fusion.10
  256.3 13.6 psum.133
  270.0 12.2 multiply_reduce_fusion.3
  282.2 8.5 psum.135
  290.7 12.9 multiply_reduce_fusion.4
  311.7 452.0 %while.31 = (s32[]{:T(128)}, f32[2048,2048]{1,0:T(8,128)}, f32[12,2048,64]{1,2,0:T(8,128)}, f32[12,2048]{1,0:T(8,128)}, f32[12,2048]{1,0:T(8,128)}, /*index=5*/b...) while((s32[]{:T(128)}, f32[2048,2048]{1,0:T(8,128)}, ...), condition=%wide.region_13.14_spmd.clone.clone, body=%wide.region_10.13_spmd.clone.sunk.clone | while | flops 1191182336 | bytes 68880512 | solution.py:163
  312.7 19.4 multiply_reduce_fusion.18
  335.1 12.2 fusion.143
  348.1 21.8 %multiply_reduce_fusion.18 = (f32[2048]{0:T(1024)S(1)}, f32[2048]{0:T(1024)S(1)}, f32[2048,2048]{1,0:T(8,128)}) fusion(f32[2048,2048]{1,0:T(8,128)} %get-tuple-element.549, f32[2048]{0:T(1024)S(1)} %bitcast.181, f32[2048,2048]{1,0:T(8,128)} %get-tuple-element.530, pred[]{:T(512)S(6)} %compare.26, f32[2048]{0:T(1024)S(1)} %bitcast.191, ...), kind=kOutput, calls=%fused_computation.27.clone.1.clone | convolution fusion | flops 608169984 | bytes 51176448 | tf_op jit(solution)/shard_map/while/body/eval_jaxpr/dot_general | solution.py:25
  373.0 12.2 fusion.143
  386.0 21.8 %multiply_reduce_fusion.18 = (f32[2048]{0:T(1024)S(1)}, f32[2048]{0:T(1024)S(1)}, f32[2048,2048]{1,0:T(8,128)}) fusion(f32[2048,2048]{1,0:T(8,128)} %get-tuple-element.549, f32[2048]{0:T(1024)S(1)} %bitcast.181, f32[2048,2048]{1,0:T(8,128)} %get-tuple-element.530, pred[]{:T(512)S(6)} %compare.26, f32[2048]{0:T(1024)S(1)} %bitcast.191, ...), kind=kOutput, calls=%fused_computation.27.clone.1.clone | convolution fusion | flops 608169984 | bytes 51176448 | tf_op jit(solution)/shard_map/while/body/eval_jaxpr/dot_general | solution.py:25
  410.8 12.2 fusion.143
  423.9 21.8 %multiply_reduce_fusion.18 = (f32[2048]{0:T(1024)S(1)}, f32[2048]{0:T(1024)S(1)}, f32[2048,2048]{1,0:T(8,128)}) fusion(f32[2048,2048]{1,0:T(8,128)} %get-tuple-element.549, f32[2048]{0:T(1024)S(1)} %bitcast.181, f32[2048,2048]{1,0:T(8,128)} %get-tuple-element.530, pred[]{:T(512)S(6)} %compare.26, f32[2048]{0:T(1024)S(1)} %bitcast.191, ...), kind=kOutput, calls=%fused_computation.27.clone.1.clone | convolution fusion | flops 608169984 | bytes 51176448 | tf_op jit(solution)/shard_map/while/body/eval_jaxpr/dot_general | solution.py:25
  448.7 12.2 fusion.143
  461.8 21.8 %multiply_reduce_fusion.18 = (f32[2048]{0:T(1024)S(1)}, f32[2048]{0:T(1024)S(1)}, f32[2048,2048]{1,0:T(8,128)}) fusion(f32[2048,2048]{1,0:T(8,128)} %get-tuple-element.549, f32[2048]{0:T(1024)S(1)} %bitcast.181, f32[2048,2048]{1,0:T(8,128)} %get-tuple-element.530, pred[]{:T(512)S(6)} %compare.26, f32[2048]{0:T(1024)S(1)} %bitcast.191, ...), kind=kOutput, calls=%fused_computation.27.clone.1.clone | convolution fusion | flops 608169984 | bytes 51176448 | tf_op jit(solution)/shard_map/while/body/eval_jaxpr/dot_general | solution.py:25
  486.5 12.2 fusion.143
  499.6 21.8 %multiply_reduce_fusion.18 = (f32[2048]{0:T(1024)S(1)}, f32[2048]{0:T(1024)S(1)}, f32[2048,2048]{1,0:T(8,128)}) fusion(f32[2048,2048]{1,0:T(8,128)} %get-tuple-element.549, f32[2048]{0:T(1024)S(1)} %bitcast.181, f32[2048,2048]{1,0:T(8,128)} %get-tuple-element.530, pred[]{:T(512)S(6)} %compare.26, f32[2048]{0:T(1024)S(1)} %bitcast.191, ...), kind=kOutput, calls=%fused_computation.27.clone.1.clone | convolution fusion | flops 608169984 | bytes 51176448 | tf_op jit(solution)/shard_map/while/body/eval_jaxpr/dot_general | solution.py:25
  524.4 12.2 fusion.143
  537.5 21.8 %multiply_reduce_fusion.18 = (f32[2048]{0:T(1024)S(1)}, f32[2048]{0:T(1024)S(1)}, f32[2048,2048]{1,0:T(8,128)}) fusion(f32[2048,2048]{1,0:T(8,128)} %get-tuple-element.549, f32[2048]{0:T(1024)S(1)} %bitcast.181, f32[2048,2048]{1,0:T(8,128)} %get-tuple-element.530, pred[]{:T(512)S(6)} %compare.26, f32[2048]{0:T(1024)S(1)} %bitcast.191, ...), kind=kOutput, calls=%fused_computation.27.clone.1.clone | convolution fusion | flops 608169984 | bytes 51176448 | tf_op jit(solution)/shard_map/while/body/eval_jaxpr/dot_general | solution.py:25
  562.2 12.2 fusion.143
  575.3 21.8 %multiply_reduce_fusion.18 = (f32[2048]{0:T(1024)S(1)}, f32[2048]{0:T(1024)S(1)}, f32[2048,2048]{1,0:T(8,128)}) fusion(f32[2048,2048]{1,0:T(8,128)} %get-tuple-element.549, f32[2048]{0:T(1024)S(1)} %bitcast.181, f32[2048,2048]{1,0:T(8,128)} %get-tuple-element.530, pred[]{:T(512)S(6)} %compare.26, f32[2048]{0:T(1024)S(1)} %bitcast.191, ...), kind=kOutput, calls=%fused_computation.27.clone.1.clone | convolution fusion | flops 608169984 | bytes 51176448 | tf_op jit(solution)/shard_map/while/body/eval_jaxpr/dot_general | solution.py:25
  600.1 12.2 fusion.143
  613.2 21.8 %multiply_reduce_fusion.18 = (f32[2048]{0:T(1024)S(1)}, f32[2048]{0:T(1024)S(1)}, f32[2048,2048]{1,0:T(8,128)}) fusion(f32[2048,2048]{1,0:T(8,128)} %get-tuple-element.549, f32[2048]{0:T(1024)S(1)} %bitcast.181, f32[2048,2048]{1,0:T(8,128)} %get-tuple-element.530, pred[]{:T(512)S(6)} %compare.26, f32[2048]{0:T(1024)S(1)} %bitcast.191, ...), kind=kOutput, calls=%fused_computation.27.clone.1.clone | convolution fusion | flops 608169984 | bytes 51176448 | tf_op jit(solution)/shard_map/while/body/eval_jaxpr/dot_general | solution.py:25
  637.9 12.2 fusion.143
  651.0 21.8 %multiply_reduce_fusion.18 = (f32[2048]{0:T(1024)S(1)}, f32[2048]{0:T(1024)S(1)}, f32[2048,2048]{1,0:T(8,128)}) fusion(f32[2048,2048]{1,0:T(8,128)} %get-tuple-element.549, f32[2048]{0:T(1024)S(1)} %bitcast.181, f32[2048,2048]{1,0:T(8,128)} %get-tuple-element.530, pred[]{:T(512)S(6)} %compare.26, f32[2048]{0:T(1024)S(1)} %bitcast.191, ...), kind=kOutput, calls=%fused_computation.27.clone.1.clone | convolution fusion | flops 608169984 | bytes 51176448 | tf_op jit(solution)/shard_map/while/body/eval_jaxpr/dot_general | solution.py:25
  675.8 12.2 fusion.143
  688.9 21.8 %multiply_reduce_fusion.18 = (f32[2048]{0:T(1024)S(1)}, f32[2048]{0:T(1024)S(1)}, f32[2048,2048]{1,0:T(8,128)}) fusion(f32[2048,2048]{1,0:T(8,128)} %get-tuple-element.549, f32[2048]{0:T(1024)S(1)} %bitcast.181, f32[2048,2048]{1,0:T(8,128)} %get-tuple-element.530, pred[]{:T(512)S(6)} %compare.26, f32[2048]{0:T(1024)S(1)} %bitcast.191, ...), kind=kOutput, calls=%fused_computation.27.clone.1.clone | convolution fusion | flops 608169984 | bytes 51176448 | tf_op jit(solution)/shard_map/while/body/eval_jaxpr/dot_general | solution.py:25
  713.7 12.2 fusion.143
  726.8 21.8 %multiply_reduce_fusion.18 = (f32[2048]{0:T(1024)S(1)}, f32[2048]{0:T(1024)S(1)}, f32[2048,2048]{1,0:T(8,128)}) fusion(f32[2048,2048]{1,0:T(8,128)} %get-tuple-element.549, f32[2048]{0:T(1024)S(1)} %bitcast.181, f32[2048,2048]{1,0:T(8,128)} %get-tuple-element.530, pred[]{:T(512)S(6)} %compare.26, f32[2048]{0:T(1024)S(1)} %bitcast.191, ...), kind=kOutput, calls=%fused_computation.27.clone.1.clone | convolution fusion | flops 608169984 | bytes 51176448 | tf_op jit(solution)/shard_map/while/body/eval_jaxpr/dot_general | solution.py:25
  751.5 12.2 fusion.143
  763.7 12.9 fusion.63
  776.6 14.0 fusion.67
  804.0 9.6 bitcast_add_fusion
  820.1 16.0 multiply_reduce_fusion.8
  844.5 8.0 fusion.98
  852.6 8.6 fusion.97
  861.4 11.3 add_add_fusion
  872.7 11.5 fusion.89
  884.2 6.9 multiply_reduce_fusion.15
  902.1 10.3 fusion.100
  919.5 7.3 fusion.88
  929.1 802.4 %all-reduce.33.cloned.1.call-done = (f32[2048,1536]{1,0:T(8,128)}, f32[2048,1536]{1,0:T(8,128)}) async-done(((f32[2048,1536]{1,0:T(8,128)}, f32[2048,1536]{1,0:T(8,128)}), (f32[2048,1536]{1,0:T(8,128)}, f32[2048,1536]{1,0:T(8,128)})) %all-reduce.33.cloned.1.call-update) | async-done | bytes 25165840 | tf_op jit(solution)/shard_map/psum | solution.py:137
  1734.9 26.1 %all-reduce.22 = (f32[384]{0:T(512)}, f32[4,768]{1,0:T(4,128)}, f32[768]{0:T(1024)}, f32[4,256]{1,0:T(4,128)}, f32[256]{0:T(256)}, /*index=5*/f32[12]{0:T(128)}, f32[12]{0:T(128)}, f32[12]{0:T(128)}, f32[768]{0:T(1024)}) all-reduce(f32[384]{0:T(512)S(1)} %multiply_reduce_fusion.11, ...), channel_id=1, replica_groups=mesh['dp'=8,'tensor'=4] {'dp'}, use_global_device_ids=true, to_apply=%region_20.21 | all-reduce | flops 6308 | bytes 50464 | tf_op jit(solution)/shard_map/psum | solution.py:237
  1760.9 8.8 multiply_reduce_fusion.2
  1769.7 20.5 %add_convert_fusion = (bf16[2048,1536]{1,0:T(8,128)(2,1)}, bf16[2048,1536]{1,0:T(8,128)(2,1)}) fusion(bf16[2048,1536]{1,0:T(8,128)(2,1)} %param.37, f32[2048,1536]{1,0:T(8,128)} %get-tuple-element.279, bf16[2048,1536]{1,0:T(8,128)(2,1)} %param.21, f32[2048]{0:T(1024)S(1)} %broadcast_multiply_fusion.2, f32[1536]{0:T(1024)S(1)} %copy-done.33, ...), kind=kLoop, calls=%fused_computation.48 | loop fusion | flops 34603008 | bytes 50354176 | tf_op jit(solution)/shard_map/convert_element_type | solution.py:221
  1790.2 142.5 %all-reduce.31.cloned.1.call-done = (f32[1536,768]{1,0:T(8,128)}, f32[1536,768]{1,0:T(8,128)}, f32[384,256]{1,0:T(8,128)}, f32[1536,12]{0,1:T(8,128)}, f32[768,1536]{1,0:T(8,128)}) async-done(((f32[1536,768]{1,0:T(8,128)}, f32[1536,768]{1,0:T(8,128)}, f32[384,256]{1,0:T(8,128)}, f32[1536,12]{0,1:T(8,128)}, f32[768,1536]{1,0:T(8,128)}), (f32[1536,768]{1,0:T(8,128)}, f32[1536,768]{1,0:T(8,128)}, ...) | async-done | bytes 14622736 | tf_op jit(solution)/shard_map/psum | solution.py:237
  (295 shorter events, 165.4 us)
Async XLA Ops:
  7.2 262.8 %copy-start = (bf16[768,1536]{1,0:T(8,128)(2,1)S(1)}, bf16[768,1536]{1,0:T(8,128)(2,1)}, u32[]{:S(2)}) copy-start(bf16[768,1536]{1,0:T(8,128)(2,1)} %param.36) | copy-start | bytes 7077892
  7.2 877.0 %all-reduce.29.cloned.1.call-start = ((), (), s32[]{:S(2)}) async-start(), calls=%async_computation | async-start | bytes 4194304 | tf_op jit(solution)/shard_map/psum | solution.py:184
  11.5 11.2 copy-start.26
  11.6 19.4 copy-start.34
  11.6 19.4 copy-start.36
  11.6 19.4 copy-start.38
  11.6 19.4 copy-start.40
  22.7 8.2 copy-start.28
  22.7 8.3 copy-start.60
  30.9 7.7 copy-start.2
  31.0 29.0 %copy-start.15 = (f32[2048]{0:T(1024)}, f32[2048]{0:T(1024)S(1)}, u32[]{:S(2)}) copy-start(f32[2048]{0:T(1024)S(1)} %get-tuple-element.311) | copy-start | bytes 24580
  31.0 29.0 %copy-start.17 = (f32[2048]{0:T(1024)}, f32[2048]{0:T(1024)S(1)}, u32[]{:S(2)}) copy-start(f32[2048]{0:T(1024)S(1)} %get-tuple-element.312) | copy-start | bytes 24580
  31.0 29.0 %copy-start.19 = (f32[2048]{0:T(1024)}, f32[2048]{0:T(1024)S(1)}, u32[]{:S(2)}) copy-start(f32[2048]{0:T(1024)S(1)} %get-tuple-element.313) | copy-start | bytes 24580
  48.6 6.6 copy-start.12
  59.9 12.6 copy-start.46
  59.9 12.6 copy-start.48
  59.9 12.6 copy-start.50
  59.9 12.6 copy-start.52
  61.2 11.4 slice-start
  64.4 8.2 copy-start.3
  64.4 8.2 copy-start.66
  64.4 8.2 slice-start.1
  64.4 8.2 copy-start.24
  64.4 8.2 copy-start.61
  72.6 9.9 copy-start.54
  82.5 147.0 %copy-start.62 = (f32[12]{0:T(128)S(1)}, f32[12]{0:T(128)}, u32[]{:S(2)}) copy-start(f32[12]{0:T(128)} %param.34) | copy-start | bytes 148
  229.5 9.5 copy-start.21
  229.5 9.5 copy-start.23
  245.6 24.3 %copy-start.56 = (f32[768]{0:T(1024)S(1)}, f32[768]{0:T(1024)}, u32[]{:S(2)}) copy-start(f32[768]{0:T(1024)} %param.35) | copy-start | bytes 9220
  269.9 20.8 %copy-start.42 = (f32[2048]{0:T(1024)}, f32[2048]{0:T(1024)S(1)}, u32[]{:S(2)}) copy-start(f32[2048]{0:T(1024)S(1)} %get-tuple-element.310) | copy-start | bytes 24580
  311.7 452.0 %copy-start.4 = (bf16[2048,256]{1,0:T(8,128)(2,1)S(1)}, bf16[2048,256]{1,0:T(8,128)(2,1)}, u32[]{:S(2)}) copy-start(bf16[2048,256]{1,0:T(8,128)(2,1)} %copy-done.3) | copy-start | bytes 3145732
  763.7 12.9 copy-start.1
  792.1 11.9 copy-start.63
  792.1 939.4 %all-reduce.33.cloned.1.call-start = ((), (), s32[]{:S(2)}) async-start(), calls=%async_computation.2 | async-start | bytes 50331648 | tf_op jit(solution)/shard_map/psum | solution.py:137
  813.5 6.6 copy-start.18
  813.5 6.6 copy-start.20
  820.1 16.1 copy-start.35
  820.1 16.1 copy-start.37
  820.1 16.1 copy-start.39
  844.5 8.0 copy-start.10
  844.5 8.0 copy-start.8
  844.5 8.0 copy-start.65
  852.5 8.6 copy-start.14
  852.5 8.6 copy-start.30
  852.6 8.6 copy-start.55
  852.6 8.8 copy-start.25
  861.4 11.3 copy-start.43
  861.4 11.3 copy-start.57
  884.2 7.0 copy-start.49
  884.2 7.0 copy-start.51
  884.2 7.0 copy-start.53
  897.5 1035.2 %all-reduce.31.cloned.1.call-start = ((), (), s32[]{:S(2)}) async-start(), calls=%async_computation.1 | async-start | bytes 29294592 | tf_op jit(solution)/shard_map/psum | solution.py:237
  897.6 14.9 slice-start.2
  902.1 10.4 slice-start.3
  902.1 10.4 copy-start.9
  902.1 17.3 slice-start.4
  902.1 17.3 slice-start.6
  912.4 7.0 slice-start.5
  912.5 7.0 slice-start.7
  912.5 7.0 copy-start.7
  928.2 806.7 %copy-start.58 = (f32[768]{0:T(1024)S(1)}, f32[768]{0:T(1024)}, u32[]{:S(2)}) copy-start(f32[768]{0:T(1024)} %get-tuple-element.212) | copy-start | bytes 9220
  928.2 832.7 %copy-start.27 = (f32[2048]{0:T(1024)S(1)}, f32[2048]{0:T(1024)}, u32[]{:S(2)}) copy-start(f32[2048]{0:T(1024)} %copy-done.26) | copy-start | bytes 24580
  928.2 832.7 %copy-start.33 = (f32[1536]{0:T(1024)S(1)}, f32[1536]{0:T(1024)}, u32[]{:S(2)}) copy-start(f32[1536]{0:T(1024)} %param.23) | copy-start | bytes 18436
  1932.7 9.7 slice-start.8
  (17 other events, 61.5 us)
Sparse Core Ops, SparseCore 0:
  792.2 86.2 all-reduce.28
  897.6 833.8 all-reduce.32
  1737.0 195.6 all-reduce.30
where the time goes:
time: 1960 us; the launch traced here: 1950 us
  waiting for transfers between devices  945 us (48%)
  matrix products  698 us (36%)
  other arithmetic  133 us (7%)
  local copies, waits for them, and re-layouts  111 us (6%)
  blocking collectives  48.2 us (2%)
    psum x1, waiting for transfers between devices, on_device(): summed = lax.psum(fast(gate_out, out_weight), 'tensor')  802 us
    dot_general x18, matrix products, against_rows(): lax.dot_general(left, right, (((1,), (1,)), ((), ())), preferred_element_...  311 us
    dot_general x17, matrix products, fast(): return jnp.dot(left, right, preferred_element_type=jnp.float32)  184 us
    dot_general x17, matrix products, contract_rows(): lax.dot_general(left, right, (((0,), (0,)), ((), ())), preferred_element_...  177 us
    psum x1, waiting for transfers between devices, on_device(): lax.psum((norm_gain_grad, gate_weight_grad, input_weight_grad, state_weig...  143 us
  transfers between devices with their start and end apart: 3, of which 2 were waited for; matrix products, arithmetic and copies ran while one was open for 8% of the time, Pallas kernels for 0%

commit v1 on v0

v1 whole, which is shorter than its diff:
```python
import functools

import jax
import jax.numpy as jnp
from jax import lax
from jax.experimental import pallas as pl
from jax.experimental.pallas import tpu as pltpu
from jax.sharding import PartitionSpec as P

epsilon = 1e-05
highest = lax.Precision.HIGHEST
f32 = jnp.float32
bf16 = jnp.bfloat16
LOG2E = 1.4426950408889634
CHUNK = 128
LANES = 128
ROWS = 512
VMEM_BYTES = 60 * 1024 * 1024
BRIEF = pl.CostEstimate(flops=1000, bytes_accessed=1000, transcendentals=0)


def dot(left, right, precision=None):
    return lax.dot_general(
        left, right, (((1,), (0,)), ((), ())), precision=precision, preferred_element_type=f32
    )


def dot_nt(left, right):
    return lax.dot_general(left, right, (((1,), (1,)), ((), ())), preferred_element_type=f32)


def dot_tn(left, right):
    return lax.dot_general(left, right, (((0,), (0,)), ((), ())), preferred_element_type=f32)


def sigmoid(values):
    return 0.5 * jnp.tanh(0.5 * values) + 0.5


def softplus(values):
    power = jnp.exp(-jnp.abs(values))
    above = 1.0 + power
    exact = above == 1.0
    tail = jnp.log(above) * (power / jnp.where(exact, 1.0, above - 1.0))
    return jnp.maximum(values, 0.0) + jnp.where(exact, power, tail)


def spread(column):
    return jnp.broadcast_to(column, (column.shape[0], LANES))


def stand(row):
    return jnp.transpose(jnp.broadcast_to(row, (CHUNK, CHUNK)))


def fold(values):
    return jnp.sum(values.reshape(values.shape[0] // 8, 8, values.shape[1]), axis=0)


def halves(values):
    upper = values.astype(bf16)
    lower = (values - upper.astype(f32)).astype(bf16)
    return jnp.concatenate([upper, lower], axis=1)


def place(axis):
    return lax.broadcasted_iota(jnp.int32, (CHUNK, CHUNK), axis)


def low_lanes():
    return place(1) < LANES // 2


def column_step(width):
    return 256 if width % 256 == 0 else 128


def conv_pre(window, taps, lanes, kept):
    total = taps[4:5, lanes] + taps[0:1, lanes] * window[8:]
    for offset in range(1, 4):
        moved = window[8 - offset : 8 - offset + CHUNK]
        total = total + taps[offset : offset + 1, lanes] * (kept[offset - 1] * moved)
    return total


def step_levels(step_raw, heads):
    field = step_raw + heads[0:1, :]
    step = softplus(field)
    tri = (place(0) >= place(1)).astype(f32)
    levels = dot(tri, step * heads[1:2, :], highest)
    return field, step, levels


HBM = pl.BlockSpec(memory_space=pl.ANY)
SMEM = pl.BlockSpec(memory_space=pltpu.SMEM)
ANY = pl.BlockSpec(memory_space=pl.ANY)


def whole(shape):
    return pl.BlockSpec(shape, lambda i: (0,) * len(shape), pipeline_mode=pl.Buffered(1))


def held(shape):
    return pl.BlockSpec(shape, lambda i: (0,) * len(shape))


def wholes(items):
    return [whole(item.shape) for item in items]


def started(pairs, semaphores, first=0):
    copies = []
    for k, (source, target) in enumerate(pairs):
        copy = pltpu.make_async_copy(source, target, semaphores.at[first + k])
        copy.start()
        copies.append(copy)
    return copies


def settle(copies):
    for copy in copies:
        copy.wait()


def line_of(values):
    return values[...].reshape(1, values.shape[0])


def prepare_kernel(
    segments,
    norm_gain,
    mixer_conv,
    mixer_shift,
    state_conv,
    state_shift,
    step_bias,
    decay_log,
    skip_gain,
    gate_gain,
    state_weight,
    step_weight,
    gain,
    marks,
    chan,
    state_chan,
    heads,
    small_weight,
):
    length = segments.shape[0]
    inner = gate_gain.shape[0]
    count = step_bias.shape[0]
    gain[...] = line_of(norm_gain)
    place_line = lax.broadcasted_iota(jnp.int32, (8, length), 1)
    first = lax.axis_index("dp") * length
    start = jnp.broadcast_to(line_of(segments), (8, length)) - first
    left = jnp.zeros((8, length), f32)
    for k in range(1, 4):
        later = pltpu.roll(start, length - k, 1)
        same = (later <= place_line) & (place_line < length - k)
        left += same.astype(f32)
    marks[0:1, :] = start[0:1].astype(f32)
    marks[1:2, :] = left[0:1]
    heads[...] = jnp.zeros_like(heads)
    rates = -jnp.exp(line_of(decay_log))
    heads[0:1, :count] = line_of(step_bias)
    heads[1:2, :count] = rates * LOG2E
    heads[2:3, :count] = rates
    heads[3:4, :count] = line_of(skip_gain)
    chan[...] = jnp.zeros_like(chan)
    chan[0:4, :] = mixer_conv[...]
    chan[4:5, :] = line_of(mixer_shift)
    owner = lax.broadcasted_iota(jnp.int32, (LANES, inner), 0)
    channel = lax.broadcasted_iota(jnp.int32, (LANES, inner), 1)
    owns = (channel // (inner // count) == owner).astype(f32)
    chan[5:6, :] = dot(heads[...], owns, highest)[3:4]
    chan[6:7, :] = line_of(gate_gain)
    state_chan[...] = jnp.zeros_like(state_chan)
    state_chan[0:4, :] = state_conv[...]
    state_chan[4:5, :] = line_of(state_shift)
    small_weight[:, :256] = state_weight[...]
    small_weight[:, 256:] = jnp.zeros((small_weight.shape[0], LANES), bf16)
    small_weight[:, 256 : 256 + count] = step_weight[...]


def prepare(length, width, inner, values):
    shapes = [
        ((1, width), f32),
        ((2, length), f32),
        ((8, inner), f32),
        ((8, 256), f32),
        ((8, LANES), f32),
        ((width, 384), bf16),
    ]
    return pl.pallas_call(
        prepare_kernel,
        grid=(1,),
        in_specs=wholes(values),
        out_specs=[whole(shape) for shape, _ in shapes],
        out_shape=[jax.ShapeDtypeStruct(shape, kind) for shape, kind in shapes],
        compiler_params=pltpu.CompilerParams(vmem_limit_bytes=VMEM_BYTES),
        cost_estimate=BRIEF,
        name="prepare",
    )(*values)


def forward_kernel(
    starts,
    marks,
    tokens_home,
    grads_home,
    input_home,
    gate_home,
    small_home,
    out_home,
    gain,
    chan,
    state_chan,
    heads,
    *rest,
    block,
    first,
    unread,
    project,
):
    if not first:
        state_in, halo_in = rest[:2]
        rest = rest[2:]
    rest = rest[unread:]
    homes, rest = rest[:11], rest[11:]
    (
        partial,
        sums,
        state,
        halo_out,
        tokens,
        grads,
        normed,
        gate_raw,
        mixer_raw,
        small_raw,
        mixer_in,
        slope,
        states,
        state_slope,
        mixed,
        back,
        kept_states,
        raw,
        state_raw,
        gated_low,
        wide_back,
        input_weight,
        gate_weight,
        state_weight,
        out_weight,
        damped,
        carried_out,
        load_sems,
        store_sems,
    ) = rest
    rows, width = tokens.shape
    inner = gate_weight.shape[1]
    wide = column_step(inner)
    here = pl.ds(block * rows, rows)
    sequence = lax.axis_index("dp") * starts.shape[0]
    loads = started(
        [
            (tokens_home.at[here, :], tokens),
            (small_home, state_weight),
            (input_home, input_weight),
            (gate_home, gate_weight),
            (grads_home.at[here, :], grads),
            (out_home, out_weight),
        ],
        load_sems,
    )
    if first:
        state[...] = jnp.zeros_like(state)
        raw[0:8, :] = jnp.zeros((8, inner), f32)
        state_raw[0:8, :] = jnp.zeros((8, 256), f32)
    else:
        state[...] = state_in[...]
        raw[0:8, :] = halo_in[:, :inner]
        state_raw[0:8, :] = halo_in[:, inner:]

    def norm_rows(index, carry):
        at = pl.ds(pl.multiple_of(index * 16, 16), 16)
        values = tokens[at, :].astype(f32)
        inverse = lax.rsqrt(jnp.mean(values * values, axis=-1, keepdims=True) + epsilon)
        normed[at, :] = (values * inverse * gain[...]).astype(bf16)
        return carry

    settle(loads[:1])
    lax.fori_loop(0, rows // 16, norm_rows, 0, unroll=4)
    stores = started([(normed, homes[0].at[here, :])], store_sems, 0)
    settle(loads[1:2])
    small = dot(normed[...], state_weight[...]).astype(bf16)
    small_raw[...] = small
    state_raw[8 : 8 + rows, :] = small[:, :256].astype(f32)
    settle(loads[2:4])
    for start in range(0, inner, wide):
        lanes = slice(start, start + wide)
        low = dot(normed[...], input_weight[:, lanes]).astype(bf16)
        mixer_raw[:, lanes] = low
        raw[8 : 8 + rows, lanes] = low.astype(f32)
        gate_raw[:, lanes] = dot(normed[...], gate_weight[:, lanes]).astype(bf16)
    settle(loads[4:])
    for start in range(0, inner, wide):
        lanes = slice(start, start + wide)
        wide_back[:, lanes] = dot_nt(grads[...], out_weight[lanes, :])

    stores += started(
        [
            (gate_raw, homes[1].at[here, :]),
            (mixer_raw, homes[2].at[here, :]),
            (small_raw, homes[3].at[here, :]),
        ],
        store_sems,
        1,
    )

    def chunk(index, carry):
        first_row = pl.multiple_of(index * CHUNK, CHUNK)
        at = pl.ds(first_row, CHUNK)
        first_token = block * rows + index * CHUNK
        chunk_first = first_token.astype(f32)
        row_place = place(0).astype(f32) + chunk_first
        lane_place = place(1).astype(f32) + chunk_first
        start_column = stand(marks[0:1, pl.ds(pl.multiple_of(block * rows + index * CHUNK, CHUNK), CHUNK)])
        age = row_place - start_column
        kept = [(age >= k).astype(f32) for k in range(1, 4)]
        for j in range(2):
            lanes = slice(j * LANES, (j + 1) * LANES)
            pre = conv_pre(
                state_raw[pl.ds(first_row, CHUNK + 8), lanes], state_chan, lanes, kept
            )
            sigma = sigmoid(pre)
            act = pre * sigma
            states[at, lanes] = act.astype(bf16)
            state_slope[at, lanes] = (sigma + act * (1.0 - sigma)).astype(bf16)
        state_b = states[at, :LANES]
        state_c = states[at, LANES:]
        scores = jnp.where(
            (lane_place <= row_place) & (lane_place >= start_column),
            dot_nt(state_c, state_b),
            0.0,
        )
        _, step_size, levels = step_levels(small_raw[at, 256:].astype(f32), heads)
        levels_row = jnp.transpose(levels)
        last_start = (starts[first_token + CHUNK - 1] - sequence).astype(f32)
        carried = (last_start < chunk_first).astype(f32)
        ends = (row_place >= last_start).astype(f32)
        begins = (start_column < chunk_first).astype(f32)
        state_low = state[...].astype(bf16)
        kept_states[index] = state_low
        carried_out[...] = dot(state_c, state_low)
        low = low_lanes()
        squares = jnp.zeros((CHUNK, LANES), f32)
        crosses = jnp.zeros((CHUNK, LANES), f32)
        for j in range(inner // LANES):
            lanes = slice(j * LANES, (j + 1) * LANES)
            pre = conv_pre(raw[pl.ds(first_row, CHUNK + 8), lanes], chan, lanes, kept)
            sigma = sigmoid(pre)
            act = pre * sigma
            value = act.astype(bf16)
            mixer_in[at, lanes] = value
            slope[at, lanes] = (sigma + act * (1.0 - sigma)).astype(bf16)
            value = value.astype(f32)
            level_pair = []
            weights = []
            for h in (2 * j, 2 * j + 1):
                level = spread(levels[:, h : h + 1])
                level_pair.append(level)
                damping = jnp.exp2(jnp.minimum(level - levels_row[h : h + 1, :], 0.0))
                weights.append((scores * damping).astype(bf16))
            level = jnp.where(low, level_pair[0], level_pair[1])
            step_pair = jnp.where(
                low,
                spread(step_size[:, 2 * j : 2 * j + 1]),
                spread(step_size[:, 2 * j + 1 : 2 * j + 2]),
            )
            stepped = value * step_pair
            stacked = jnp.concatenate(
                [jnp.where(low, stepped, 0.0), jnp.where(low, 0.0, stepped)], axis=0
            ).astype(bf16)
            end_level = level[CHUNK - 1 : CHUNK, :]
            result = dot(jnp.concatenate(weights, axis=1), stacked)
            result += (begins * jnp.exp2(level)) * carried_out[:, lanes]
            damped[:, lanes] = (stepped * (ends * jnp.exp2(end_level - level))).astype(bf16)
            state[:, lanes] = state[:, lanes] * (carried * jnp.exp2(end_level))
            result += chan[5:6, lanes] * value
            mixed[at, lanes] = result
            gate = gate_raw[at, lanes].astype(f32)
            gated = result * (gate * sigmoid(gate))
            squares += gated * gated
            gained = gated * chan[6:7, lanes]
            gated_low[at, lanes] = gained.astype(bf16)
            out_back = wide_back[at, lanes]
            back[at, lanes] = out_back.astype(bf16)
            crosses += out_back * gained
        state[...] += dot_tn(state_b, damped[...])
        sums[0:1, at] = jnp.sum(jnp.transpose(squares), axis=0, keepdims=True)
        sums[1:2, at] = jnp.sum(jnp.transpose(crosses), axis=0, keepdims=True)
        return carry

    lax.fori_loop(0, rows // CHUNK, chunk, 0)
    stores += started(
        [
            (mixer_in, homes[4].at[here, :]),
            (slope, homes[5].at[here, :]),
            (states, homes[6].at[here, :]),
            (state_slope, homes[7].at[here, :]),
            (mixed, homes[8].at[here, :]),
            (back, homes[9].at[here, :]),
            (kept_states, homes[10].at[pl.ds(block * (rows // CHUNK), rows // CHUNK)]),
        ],
        store_sems,
        4,
    )
    if project:
        for start in range(0, width, 512):
            lanes = slice(start, start + 512)
            partial[:, lanes] = dot(gated_low[...], out_weight[:, lanes]).astype(bf16)
    else:
        partial[...] = gated_low[...]
    halo_out[:, :inner] = raw[rows : rows + 8, :]
    halo_out[:, inner:] = state_raw[rows : rows + 8, :]
    settle(stores)


def forward(block, starts, marks, tokens, grads, params, carry, earlier, after, project):
    gain, gate_weight, input_weight, small_weight, chan, state_chan, heads, out_weight = params
    tables = [gain, chan, state_chan, heads]
    weights = [input_weight, gate_weight, small_weight, out_weight]
    length, width = tokens.shape
    inner = gate_weight.shape[1]
    chunks = ROWS // CHUNK
    stored = [
        (width, bf16),
        (inner, bf16),
        (inner, bf16),
        (384, bf16),
        (inner, bf16),
        (inner, bf16),
        (256, bf16),
        (256, bf16),
        (inner, f32),
        (inner, bf16),
    ]
    out_shape = [jax.ShapeDtypeStruct((length, columns), kind) for columns, kind in stored]
    out_shape += [jax.ShapeDtypeStruct((length // CHUNK, LANES, inner), bf16)]
    shared = len(out_shape)
    own = [
        ((ROWS, width if project else inner), bf16),
        ((2, ROWS), f32),
        ((LANES, inner), f32),
        ((8, inner + 256), f32),
    ]
    out_shape += [jax.ShapeDtypeStruct(shape, kind) for shape, kind in own]
    in_specs = [SMEM, whole(marks.shape)] + [HBM] * 6 + wholes(tables) + wholes(carry)
    operands = [starts, marks, tokens, grads, *weights, *tables, *carry]
    aliases = {}
    if earlier is not None:
        aliases = {len(operands) + k: k for k in range(shared)}
        in_specs += [HBM] * shared
        operands += list(earlier)
    operands += list(after)
    in_specs += [ANY] * len(after)
    outs = pl.pallas_call(
        functools.partial(
            forward_kernel,
            block=block,
            first=not carry,
            unread=len(aliases) + len(after),
            project=project,
        ),
        grid=(1,),
        in_specs=in_specs,
        out_specs=[HBM] * shared + [whole(shape) for shape, _ in own],
        out_shape=out_shape,
        scratch_shapes=[
            pltpu.VMEM((ROWS, width), bf16),
            pltpu.VMEM((ROWS, width), bf16),
            *[pltpu.VMEM((ROWS, columns), kind) for columns, kind in stored],
            pltpu.VMEM((chunks, LANES, inner), bf16),
            pltpu.VMEM((ROWS + 8, inner), f32),
            pltpu.VMEM((ROWS + 8, 256), f32),
            pltpu.VMEM((ROWS, inner), bf16),
            pltpu.VMEM((ROWS, inner), f32),
            *[pltpu.VMEM(item.shape, bf16) for item in weights],
            pltpu.VMEM((CHUNK, inner), bf16),
            pltpu.VMEM((CHUNK, inner), f32),
            pltpu.SemaphoreType.DMA((6,)),
            pltpu.SemaphoreType.DMA((11,)),
        ],
        input_output_aliases=aliases,
        compiler_params=pltpu.CompilerParams(vmem_limit_bytes=VMEM_BYTES),
        cost_estimate=BRIEF,
        name="forward_mix",
    )(*operands)
    saved, (partial, sums, *carry) = outs[:shared], outs[shared:]
    return saved, partial, sums, carry


def project_kernel(*refs, count, unread):
    lows, out_weight, outs = refs[:count], refs[count], refs[count + 1 + unread :]
    for low, out in zip(lows, outs):
        for start in range(0, out.shape[1], 512):
            lanes = slice(start, start + 512)
            out[:, lanes] = dot(low[...], out_weight[:, lanes]).astype(bf16)


def project_rows(lows, out_weight, after):
    width = out_weight.shape[1]
    half = lambda columns: pl.BlockSpec((ROWS // 2, columns), lambda i: (i, 0))
    return pl.pallas_call(
        functools.partial(project_kernel, count=len(lows), unread=len(after)),
        grid=(2,),
        in_specs=[half(low.shape[1]) for low in lows]
        + [whole(out_weight.shape)]
        + [ANY] * len(after),
        out_specs=[half(width)] * len(lows),
        out_shape=[jax.ShapeDtypeStruct((low.shape[0], width), bf16) for low in lows],
        compiler_params=compiler_params(),
        cost_estimate=BRIEF,
        name="project_rows",
    )(*lows, out_weight, *after)


def compiler_params():
    return pltpu.CompilerParams(
        dimension_semantics=("arbitrary",), vmem_limit_bytes=VMEM_BYTES
    )


def gate_kernel(total_inner, sums, mixed, gate_raw, back, chan, *rest, unread):
    grad_low, gate_low, gate_out, gain_sums = rest[unread:]
    inner = chan.shape[1]

    @pl.when(pl.program_id(0) == 0)
    def _():
        gain_sums[...] = jnp.zeros_like(gain_sums)

    def chunk(index, carry):
        at = pl.ds(pl.multiple_of(index * CHUNK, CHUNK), CHUNK)
        inverse = lax.rsqrt(sums[0:1, at] / total_inner + epsilon)
        rms = stand(inverse)
        pull = stand(inverse * inverse * inverse * (sums[1:2, at] / total_inner))
        for j in range(inner // LANES):
            lanes = slice(j * LANES, (j + 1) * LANES)
            gate = gate_raw[at, lanes].astype(f32)
            sigma = sigmoid(gate)
            gate_act = gate * sigma
            mix = mixed[at, lanes]
            gated = mix * gate_act
            unit = gated * rms
            out_back = back[at, lanes].astype(f32)
            gate_gain = chan[6:7, lanes]
            gain_sums[:, lanes] += fold(out_back * unit)
            gated_grad = rms * (out_back * gate_gain) - pull * gated
            gate_low[at, lanes] = (
                gated_grad * mix * (sigma + gate_act * (1.0 - sigma))
            ).astype(bf16)
            gate_out[at, lanes] = (unit * gate_gain).astype(bf16)
            grad_low[at, lanes] = (gated_grad * gate_act).astype(bf16)
        return carry

    lax.fori_loop(0, mixed.shape[0] // CHUNK, chunk, 0)


def gate_grads(total_inner, sums, mixed, gate_raw, back, chan, after):
    length, inner = mixed.shape
    rows_of = lambda columns: pl.BlockSpec((ROWS, columns), lambda i: (i, 0))
    return pl.pallas_call(
        functools.partial(gate_kernel, total_inner, unread=len(after)),
        grid=(length // ROWS,),
        in_specs=[
            pl.BlockSpec((2, ROWS), lambda i: (0, i)),
            rows_of(inner),
            rows_of(inner),
            rows_of(inner),
            whole((8, inner)),
            *[ANY] * len(after),
        ],
        out_specs=[rows_of(inner)] * 3 + [held((8, inner))],
        out_shape=[jax.ShapeDtypeStruct((length, inner), bf16)] * 3
        + [jax.ShapeDtypeStruct((8, inner), f32)],
        compiler_params=compiler_params(),
        cost_estimate=BRIEF,
        name="gate_grads",
    )(sums, mixed, gate_raw, back, chan, *after)


def backward_kernel(
    starts,
    marks,
    gain,
    chan,
    state_chan,
    heads,
    *rest,
    block,
    first,
    unread,
    parts,
):
    sources, rest = rest[:14], rest[14:]
    if not first:
        earlier, rest = rest[:6], rest[6:]
    rest = rest[unread:]
    mixer_home, small_home = rest[:2]
    partials, rest = rest[2 : 2 + parts], rest[2 + parts :]
    results, rest = rest[:6], rest[6:]
    state_grad, halo_out, chan_sums, state_sums, head_sums, gain_sums = results
    buffers, rest = rest[:14], rest[14:]
    (
        mixed,
        mixer_grad,
        mixer_in,
        slope,
        small_raw,
        states,
        state_slope,
        kept_states,
        mixer_raw,
        gate_low,
        gate_weight,
        input_weight,
        state_weight,
        tokens,
    ) = buffers
    (
        mixer_low,
        small_low,
        pre_grad,
        state_pre,
        ends_low,
        begins_low,
        normed_grad,
        picks,
        carried_back,
        load_sems,
        store_sems,
    ) = rest
    rows, width = tokens.shape
    inner = gate_weight.shape[1]
    chunks = rows // CHUNK
    half = rows // 2
    here = pl.ds(block * rows, rows)
    sequence = lax.axis_index("dp") * starts.shape[0]

    def part_of(number):
        pairs = [
            (source.at[pl.ds(block * rows + number * half, half), :], buffer.at[pl.ds(number * half, half), :])
            for source, buffer in zip(sources[:7], buffers[:7])
        ]
        count = chunks // 2
        pairs.append(
            (
                sources[7].at[pl.ds(block * chunks + number * count, count)],
                kept_states.at[pl.ds(number * count, count)],
            )
        )
        return pairs

    soon = started(part_of(1), load_sems)
    second = started(part_of(0), load_sems, 8)
    late = started(
        [
            (source if source.shape[0] == buffer.shape[0] else source.at[here, :], buffer)
            for source, buffer in zip(sources[8:], buffers[8:])
        ],
        load_sems,
        16,
    )
    for j in range(inner // LANES):
        column = lax.broadcasted_iota(jnp.int32, (2 * LANES, LANES), 1)
        line = lax.broadcasted_iota(jnp.int32, (2 * LANES, LANES), 0) % LANES
        owner = 2 * j + (line >= LANES // 2).astype(jnp.int32)
        picks[j] = (column == owner).astype(bf16)
    if first:
        for result in results:
            result[...] = jnp.zeros_like(result)
        pre_grad[rows : rows + 8, :] = jnp.zeros((8, inner), f32)
        state_pre[rows : rows + 8, :] = jnp.zeros((8, 256), f32)
    else:
        for result, value in zip(results, earlier):
            result[...] = value[...]
        pre_grad[rows : rows + 8, :] = earlier[1][:, :inner]
        state_pre[rows : rows + 8, :] = earlier[1][:, inner:]
    settle(soon)

    def chunk(turn, carry):
        index = chunks - 1 - turn

        @pl.when(turn == chunks // 2)
        def _():
            settle(second)

        first_row = pl.multiple_of(index * CHUNK, CHUNK)
        at = pl.ds(first_row, CHUNK)
        first_token = block * rows + index * CHUNK
        chunk_first = first_token.astype(f32)
        row_place = place(0).astype(f32) + chunk_first
        lane_place = place(1).astype(f32) + chunk_first
        start_row = marks[0:1, pl.ds(pl.multiple_of(block * rows + index * CHUNK, CHUNK), CHUNK)]
        start_column = stand(start_row)
        seen = (row_place <= lane_place) & (row_place >= start_row)
        last_start = (starts[first_token + CHUNK - 1] - sequence).astype(f32)
        carried = (last_start < chunk_first).astype(f32)
        ends = (row_place >= last_start).astype(f32)
        begins = (start_column < chunk_first).astype(f32)
        state_b = states[at, :LANES]
        state_c = states[at, LANES:]
        scores = jnp.where(seen, dot_nt(state_b, state_c), 0.0)
        step_raw = small_raw[at, 256:].astype(f32)
        field, step_size, levels = step_levels(step_raw, heads)
        levels_row = jnp.transpose(levels)
        state_low = state_grad[...].astype(bf16)
        carried_back[...] = dot(state_b, state_low)
        low = low_lanes()
        score_grad = jnp.zeros((CHUNK, CHUNK), f32)
        level_grad = jnp.zeros((CHUNK, LANES), f32)
        inter_grad = jnp.zeros((CHUNK, LANES), f32)
        crossing_sum = jnp.zeros((8, LANES), f32)
        step_grad = jnp.zeros((CHUNK, LANES), f32)
        for j in range(inner // LANES):
            lanes = slice(j * LANES, (j + 1) * LANES)
            pick = picks[j]
            mix = mixed[at, lanes]
            grad = mixer_grad[at, lanes].astype(f32)
            value = mixer_in[at, lanes].astype(f32)
            skip = chan[5:6, lanes]
            chan_sums[0:8, lanes] += fold(grad * value)
            step_pair = jnp.where(
                low,
                spread(step_size[:, 2 * j : 2 * j + 1]),
                spread(step_size[:, 2 * j + 1 : 2 * j + 2]),
            )
            stepped = value * step_pair
            stepped_low = stepped.astype(bf16)
            stacked = jnp.concatenate(
                [jnp.where(low, grad, 0.0), jnp.where(low, 0.0, grad)], axis=0
            ).astype(bf16)
            cells = dot_nt(stepped_low, stacked)
            level_pair = []
            weights = []
            for k in range(2):
                h = 2 * j + k
                level = spread(levels[:, h : h + 1])
                level_pair.append(level)
                damping = jnp.exp2(jnp.minimum(levels_row[h : h + 1, :] - level, 0.0))
                weights.append((scores * damping).astype(bf16))
                score_grad += cells[:, k * CHUNK : (k + 1) * CHUNK] * damping
            level = jnp.where(low, level_pair[0], level_pair[1])
            end_level = level[CHUNK - 1 : CHUNK, :]
            ending = ends * jnp.exp2(end_level - level)
            beginning = begins * jnp.exp2(level)
            within = dot(jnp.concatenate(weights, axis=1), stacked)
            beyond = ending * carried_back[:, lanes]
            value_grad = within + beyond
            ends_low[:, lanes] = (stepped * ending).astype(bf16)
            begins_low[:, lanes] = (grad * beginning).astype(bf16)
            behind = state_grad[:, lanes]
            crossing = fold(behind * kept_states[index, :, lanes].astype(f32))
            crossing_sum += dot(halves(crossing), pick)
            state_grad[:, lanes] = behind * (carried * jnp.exp2(end_level))
            rows_flow = grad * (mix - skip * value) - stepped_low.astype(f32) * within
            level_grad += dot(halves(rows_flow), pick)
            inter_grad += dot((stepped * beyond).astype(bf16), pick[:LANES])
            step_grad += dot((value * value_grad).astype(bf16), pick[:LANES])
            pre_grad[at, lanes] = (step_pair * value_grad + skip * grad) * slope[
                at, lanes
            ].astype(f32)
        state_grad[...] += dot_tn(state_c, begins_low[...])
        score_low = jnp.where(seen, score_grad, 0.0).astype(bf16)
        state_pre[at, :LANES] = (
            dot(score_low, state_c) + dot_nt(ends_low[...], state_low)
        ) * state_slope[at, :LANES].astype(f32)
        state_pre[at, LANES:] = (
            dot_tn(score_low, state_b) + dot_nt(begins_low[...], kept_states[index])
        ) * state_slope[at, LANES:].astype(f32)
        onward = (place(0) <= place(1)).astype(f32)
        before = (place(0) > place(1)).astype(f32)
        across = jnp.sum(crossing_sum, axis=0, keepdims=True) * (
            carried * jnp.exp2(levels[CHUNK - 1 : CHUNK, :])
        )
        reach = dot(onward, level_grad, highest) + dot(before, inter_grad, highest) + across
        rates = heads[2:3, :]
        field_grad = (step_grad + reach * rates) * sigmoid(field)
        small_low[at, 256:] = field_grad.astype(bf16)
        head_sums[0:8, :] += fold(field_grad)
        head_sums[8:16, :] += fold(reach * step_size * rates)
        return carry

    lax.fori_loop(0, chunks, chunk, 0)
    settle(late)

    def unconv(index, carry):
        first_row = pl.multiple_of(index * CHUNK, CHUNK)
        at = pl.ds(first_row, CHUNK)
        left = stand(marks[1:2, pl.ds(pl.multiple_of(block * rows + index * CHUNK, CHUNK), CHUNK)])
        kept = [(left >= k).astype(f32) for k in range(1, 4)]

        def tile(window, value, taps, lanes, totals, line):
            own = window[:CHUNK]
            total = taps[0:1, lanes] * own
            totals[line : line + 8, lanes] += fold(value * own)
            for k in range(1, 4):
                moved = kept[k - 1] * window[k : k + CHUNK]
                total += taps[k : k + 1, lanes] * moved
                totals[line + 8 * k : line + 8 * k + 8, lanes] += fold(value * moved)
            totals[line + 32 : line + 40, lanes] += fold(own)
            return total.astype(bf16)

        for j in range(inner // LANES):
            lanes = slice(j * LANES, (j + 1) * LANES)
            mixer_low[at, lanes] = tile(
                pre_grad[pl.ds(first_row, CHUNK + 8), lanes],
                mixer_raw[at, lanes].astype(f32),
                chan,
                lanes,
                chan_sums,
                8,
            )
        for j in range(2):
            lanes = slice(j * LANES, (j + 1) * LANES)
            small_low[at, lanes] = tile(
                state_pre[pl.ds(first_row, CHUNK + 8), lanes],
                small_raw[at, lanes].astype(f32),
                state_chan,
                lanes,
                state_sums,
                0,
            )
        return carry

    lax.fori_loop(0, chunks, unconv, 0)
    stores = started(
        [(mixer_low, mixer_home.at[here, :]), (small_low, small_home.at[here, :])], store_sems
    )
    for start in range(0, width, 256):
        lanes = slice(start, start + 256)
        normed_grad[:, lanes] = (
            dot_nt(gate_low[...], gate_weight[lanes, :])
            + dot_nt(mixer_low[...], input_weight[lanes, :])
            + dot_nt(small_low[...], state_weight[lanes, :])
        )

    def unnorm(part, index, carry):
        at = pl.ds(pl.multiple_of(index * 16, 16), 16)
        from_row = pl.ds(pl.multiple_of(part * part_rows + index * 16, 16), 16)
        values = tokens[from_row, :].astype(f32)
        inverse = lax.rsqrt(jnp.mean(values * values, axis=-1, keepdims=True) + epsilon)
        unit = values * inverse
        grad = normed_grad[from_row, :]
        gain_sums[...] += fold(grad * unit)
        grad = grad * gain[...]
        out = partials[part]
        out[at, :] = (
            inverse * (grad - unit * jnp.mean(grad * unit, axis=-1, keepdims=True))
        ).astype(bf16)
        return carry

    part_rows = partials[0].shape[0]
    for part in range(len(partials)):
        lax.fori_loop(0, part_rows // 16, functools.partial(unnorm, part), 0, unroll=2)
    halo_out[:, :inner] = pre_grad[0:8, :]
    halo_out[:, inner:] = state_pre[0:8, :]
    settle(stores)


def backward(block, starts, marks, tokens, params, saved, grads, carry, earlier, after, parts):
    gain, gate_weight, input_weight, small_weight, chan, state_chan, heads, _ = params
    tables = [gain, chan, state_chan, heads]
    length, width = tokens.shape
    inner = gate_weight.shape[1]
    chunks = ROWS // CHUNK
    (gate_raw, mixer_raw, small_raw, mixer_in, slope, states, state_slope, mixed, _, kept) = saved
    mixer_grad, gate_low = grads
    sources = [
        mixed,
        mixer_grad,
        mixer_in,
        slope,
        small_raw,
        states,
        state_slope,
        kept,
        mixer_raw,
        gate_low,
        gate_weight,
        input_weight,
        small_weight,
        tokens,
    ]
    operands = [starts, marks, *tables, *sources, *carry]
    in_specs = [SMEM, *wholes([marks, *tables]), *[HBM] * len(sources), *wholes(carry)]
    aliases = {}
    if earlier is not None:
        aliases = {len(operands) + k: k for k in range(2)}
        in_specs += [HBM] * 2
        operands += list(earlier)
    operands += list(after)
    in_specs += [ANY] * len(after)
    results = [
        (LANES, inner),
        (8, inner + 256),
        (48, inner),
        (40, 256),
        (16, LANES),
        (8, width),
    ]
    outs = pl.pallas_call(
        functools.partial(
            backward_kernel,
            block=block,
            first=not carry,
            unread=len(aliases) + len(after),
            parts=parts,
        ),
        grid=(1,),
        in_specs=in_specs,
        out_specs=[HBM] * 2
        + [whole((ROWS // parts, width))] * parts
        + [whole(shape) for shape in results],
        out_shape=[
            jax.ShapeDtypeStruct((length, inner), bf16),
            jax.ShapeDtypeStruct((length, 384), bf16),
            *[jax.ShapeDtypeStruct((ROWS // parts, width), bf16)] * parts,
            *[jax.ShapeDtypeStruct(shape, f32) for shape in results],
        ],
        scratch_shapes=[
            *[
                pltpu.VMEM((chunks, LANES, inner), bf16)
                if source.ndim == 3
                else pltpu.VMEM(
                    (ROWS if source.shape[0] == length else source.shape[0], source.shape[1]),
                    source.dtype,
                )
                for source in sources
            ],
            pltpu.VMEM((ROWS, inner), bf16),
            pltpu.VMEM((ROWS, 384), bf16),
            pltpu.VMEM((ROWS + 8, inner), f32),
            pltpu.VMEM((ROWS + 8, 256), f32),
            pltpu.VMEM((CHUNK, inner), bf16),
            pltpu.VMEM((CHUNK, inner), bf16),
            pltpu.VMEM((ROWS, width), f32),
            pltpu.VMEM((inner // LANES, 2 * LANES, LANES), bf16),
            pltpu.VMEM((CHUNK, inner), f32),
            pltpu.SemaphoreType.DMA((22,)),
            pltpu.SemaphoreType.DMA((2,)),
        ],
        input_output_aliases=aliases,
        compiler_params=pltpu.CompilerParams(vmem_limit_bytes=VMEM_BYTES),
        cost_estimate=BRIEF,
        name="backward_mix",
    )(*operands)
    return outs[:2], outs[2 : 2 + parts], outs[2 + parts :]


def pack(packed, chan_sums, gate_sums, head_sums, state_sums, gain_sums, step_lines):
    inner = chan_sums.shape[1]
    packed[...] = jnp.zeros_like(packed)
    total = lambda values: jnp.sum(values, axis=0, keepdims=True)
    for k in range(6):
        packed[k : k + 1, :inner] = total(chan_sums[8 * k : 8 * k + 8, :])
    packed[6:7, :inner] = total(gate_sums[...])
    for k in range(2):
        packed[7:8, k * LANES : (k + 1) * LANES] = total(head_sums[8 * k : 8 * k + 8, :])
    for k in range(5):
        packed[8 + k : 9 + k, :256] = total(state_sums[8 * k : 8 * k + 8, :])
    packed[13:14, :] = total(gain_sums[...])
    packed[16:32, :] = step_lines[0:16, :]


def weight_kernel(left, *rest, rights, unread, packs):
    right, rest = rest[:rights], rest[rights:]
    sums, rest = rest[:packs], rest[packs + unread :]
    outs, totals = rest[: rights + bool(packs)], rest[rights + bool(packs) :]
    step = pl.program_id(0)

    @pl.when(step == 0)
    def _():
        for total in totals:
            total[...] = jnp.zeros_like(total)

    for start in range(0, left.shape[1], 256):
        columns = slice(start, start + 256)
        for item, total in zip(right, totals):
            total[columns, :] += dot_tn(left[:, columns], item[...])
        if packs:
            totals[rights][:, columns] += dot_tn(right[-1][:, 256:], left[:, columns])

    @pl.when(step == pl.num_programs(0) - 1)
    def _():
        if packs:
            packed = totals[rights + 1]
            pack(packed, *sums, totals[rights])
            outs[rights][...] = packed[...].astype(bf16)
        for out, total in zip(outs[:rights], totals):
            out[...] = total[:, : out.shape[1]].astype(bf16)


def weight_grads(left, rights, after, sums=()):
    length, height = left.shape
    rows_of = lambda columns: pl.BlockSpec((ROWS, columns), lambda i: (i, 0))
    shapes = [(height, item.shape[1]) for item in rights]
    outs, scratch = list(shapes), list(shapes)
    if sums:
        outs[-1] = (height, 256)
        outs.append((32, height))
        scratch += [(LANES, height), (32, height)]
    return pl.pallas_call(
        functools.partial(
            weight_kernel, rights=len(rights), unread=len(after), packs=len(sums)
        ),
        grid=(length // ROWS,),
        in_specs=[rows_of(height)]
        + [rows_of(item.shape[1]) for item in rights]
        + wholes(sums)
        + [ANY] * len(after),
        out_specs=[held(shape) for shape in outs],
        out_shape=[jax.ShapeDtypeStruct(shape, bf16) for shape in outs],
        scratch_shapes=[pltpu.VMEM(shape, f32) for shape in scratch],
        compiler_params=compiler_params(),
        cost_estimate=BRIEF,
        name="weight_grads",
    )(left, *rights, *sums, *after)


def land_kernel(take, total_home, moved_home, *rest, mode, unread):
    out_home, total, moved, out, load_sems, store_sems = rest[unread:]
    tiles = total.shape[0] // CHUNK
    part = [pl.ds(k * CHUNK, CHUNK) for k in range(tiles)]
    loads = [
        started(
            [
                (total_home.at[part[k], :], total.at[part[k], :]),
                (moved_home.at[part[k], :], moved.at[part[k], :]),
            ],
            load_sems,
            2 * k,
        )
        for k in range(tiles)
    ]
    stores = []
    for k in range(tiles):
        settle(loads[k])
        at = slice(k * CHUNK, (k + 1) * CHUNK)
        if mode == "add":
            out[at, :] = total[at, :] + moved[at, :]
        else:
            out[at, :] = jnp.where(take[0] > 0, moved[at, :], total[at, :])
        stores += started([(out.at[part[k], :], out_home.at[part[k], :])], store_sems, k)
    settle(stores)


def finish_kernel(
    take, total_home, moved_home, base_home, sums, *rest, adds, inner, row, unread
):
    out_home, total, moved, base, out, load_sems, store_sems = rest[unread:]
    rows = total.shape[0]
    tiles = rows // CHUNK
    at_home = lambda k: pl.ds(row + k * CHUNK, CHUNK)
    at_here = lambda k: pl.ds(k * CHUNK, CHUNK)

    def run(pairs):
        loads = [
            started(
                [(home.at[at_here(k), :], here.at[at_here(k), :]) for home, here in pairs]
                + [(base_home.at[at_home(k), :], base.at[at_here(k), :])],
                load_sems,
                3 * k,
            )
            for k in range(tiles)
        ]
        stores = []
        for k in range(tiles):
            at = slice(k * CHUNK, (k + 1) * CHUNK)
            if inner:
                scale = stand(
                    lax.rsqrt(
                        sums[0:1, row + k * CHUNK : row + (k + 1) * CHUNK] / inner + epsilon
                    )
                )
            settle(loads[k])
            for start in range(0, total.shape[1], LANES):
                lanes = slice(start, start + LANES)
                value = pairs[0][1][at, lanes].astype(f32)
                for _, here in pairs[1:]:
                    value += here[at, lanes].astype(f32)
                if inner:
                    value = value * scale
                out[at, lanes] = (value + base[at, lanes].astype(f32)).astype(bf16)
            stores += started(
                [(out.at[at_here(k), :], out_home.at[at_home(k), :])], store_sems, k
            )
        settle(stores)

    if adds:
        run([(moved_home, moved), (total_home, total)])
        return

    @pl.when(take[0] > 0)
    def _():
        run([(moved_home, moved)])

    @pl.when(take[0] <= 0)
    def _():
        run([(total_home, total)])


def land(take, total, moved, mode, after):
    rows, width = total.shape
    return pl.pallas_call(
        functools.partial(land_kernel, mode=mode, unread=len(after)),
        in_specs=[SMEM, HBM, HBM] + [ANY] * len(after),
        out_specs=HBM,
        out_shape=jax.ShapeDtypeStruct((rows, width), bf16),
        scratch_shapes=[
            *[pltpu.VMEM((rows, width), bf16)] * 3,
            pltpu.SemaphoreType.DMA((2 * rows // CHUNK,)),
            pltpu.SemaphoreType.DMA((rows // CHUNK,)),
        ],
        compiler_params=pltpu.CompilerParams(vmem_limit_bytes=VMEM_BYTES),
        cost_estimate=BRIEF,
        name="line_land",
    )(take, total, moved, *after)


def finish(take, total, moved, adds, base, sums, inner, row, earlier, after):
    rows, width = total.shape
    operands = [take, total, moved, base, sums]
    in_specs = [SMEM, HBM, HBM, HBM, whole(sums.shape)]
    aliases = {}
    if earlier is not None:
        aliases = {len(operands): 0}
        operands += [earlier]
        in_specs += [HBM]
    after = [item for item in after if item is not earlier]
    operands += after
    in_specs += [ANY] * len(after)
    return pl.pallas_call(
        functools.partial(
            finish_kernel,
            adds=adds,
            inner=inner,
            row=row,
            unread=len(aliases) + len(after),
        ),
        in_specs=in_specs,
        out_specs=HBM,
        grid=(1,),
        out_shape=jax.ShapeDtypeStruct(base.shape, bf16),
        scratch_shapes=[
            *[pltpu.VMEM((rows, width), bf16)] * 4,
            pltpu.SemaphoreType.DMA((3 * rows // CHUNK,)),
            pltpu.SemaphoreType.DMA((rows // CHUNK,)),
        ],
        input_output_aliases=aliases,
        compiler_params=pltpu.CompilerParams(vmem_limit_bytes=VMEM_BYTES),
        cost_estimate=BRIEF,
        name="line_finish",
    )(*operands)


class Line:
    def __init__(self, members, me):
        middle = members // 2
        self.steps = [
            ("add", [(near, near + 1), (members - 1 - near, members - 2 - near)], near)
            for near in range(middle - 1)
        ]
        self.steps.append(("add", [(middle - 1, middle), (middle, middle - 1)], 0))
        self.steps += [
            ("take", [(near + 1, near), (members - 2 - near, members - 1 - near)], near)
            for near in reversed(range(middle - 1))
        ]
        self.takes = [
            ((me == near) | (me == members - 1 - near)).astype(jnp.int32)[None]
            for _, _, near in self.steps
        ]
        self.flying = [[] for _ in self.steps]
        self.outs = {}

    def push(self, total, name, row):
        self.launch(0, total, name, row)

    def launch(self, step, total, name, row):
        moved = lax.ppermute(total, "tensor", self.steps[step][1])
        self.flying[step].append((total, moved, name, row))

    def tick(self, ending, after, first=1, then=1, last=1):
        ready = []
        for step, queue in enumerate(self.flying):
            count = last if step == len(self.flying) - 1 else then if step else first
            for _ in range(min(len(queue), count)):
                ready.append((step, queue.pop(0)))
        for step, (total, moved, name, row) in ready:
            mode = self.steps[step][0]
            if step < len(self.steps) - 1:
                total = land(self.takes[step], total, moved, mode, after)
                self.launch(step + 1, total, name, row)
                after = [total]
            else:
                base, sums, inner = ending[name]
                out = finish(
                    self.takes[step],
                    total,
                    moved,
                    mode == "add",
                    base,
                    sums,
                    inner,
                    row,
                    self.outs.get(name),
                    after,
                )
                self.outs[name] = out
                after = [out]
        return after

    def busy(self):
        return any(self.flying)

    def pending(self):
        return sum(len(queue) for queue in self.flying)


def sum_over(values, axis, size):
    parts = [values]
    for k in range(1, size):
        parts.append(lax.ppermute(values, axis, [(i, i ^ k) for i in range(size)]))
    while len(parts) > 1:
        parts = [parts[k] + parts[k + 1] for k in range(0, len(parts), 2)]
    return parts[0]


def part_kernel(me, lines, values, *rest, size, unread):
    outs = rest[unread:]
    rows = values.shape[0] // size
    for k in range(size):
        first = pl.multiple_of((me[0] ^ k) * rows, 32)
        outs[k][:rows, :] = values[pl.ds(first, rows), :]
        for j in range(lines.shape[1] // 256):
            at = slice(rows + 16 * j, rows + 16 * j + 16)
            outs[k][at, :] = lines[0:16, 256 * j : 256 * j + 256]


def join_kernel(*refs):
    parts, (line_sums, value_sums) = list(refs[:-2]), refs[-2:]
    rows = value_sums.shape[0]
    for out, at in [(value_sums, slice(0, rows)), (line_sums, slice(rows, None))]:
        totals = [part[at, :].astype(f32) for part in parts]
        while len(totals) > 1:
            totals = [totals[k] + totals[k + 1] for k in range(0, len(totals), 2)]
        out[...] = totals[0]


def sum_pieces(lines, values, axis, size, me, after):
    rows = values.shape[0] // size
    height = rows + 16 * (lines.shape[1] // 256)
    shape = jax.ShapeDtypeStruct((height, 256), bf16)
    own, *sent = pl.pallas_call(
        functools.partial(part_kernel, size=size, unread=len(after)),
        grid=(1,),
        in_specs=[SMEM, *wholes([lines, values]), *[ANY] * len(after)],
        out_specs=[whole(shape.shape)] * size,
        out_shape=[shape] * size,
        compiler_params=compiler_params(),
        cost_estimate=BRIEF,
        name="part_pieces",
    )(me[None], lines, values, *after)
    parts = [own] + [
        lax.ppermute(sent[k - 1], axis, [(i, i ^ k) for i in range(size)])
        for k in range(1, size)
    ]
    outs = [(height - rows, 256), (rows, 256)]
    line_sums, value_sums = pl.pallas_call(
        join_kernel,
        grid=(1,),
        in_specs=wholes(parts),
        out_specs=[whole(item) for item in outs],
        out_shape=[jax.ShapeDtypeStruct(item, f32) for item in outs],
        compiler_params=compiler_params(),
        cost_estimate=BRIEF,
        name="join_pieces",
    )(*parts)
    return line_sums.reshape(-1, 16, 256), value_sums


def on_device(
    block_input,
    segment_ids,
    norm_gain,
    gate_weight,
    input_weight,
    state_weight,
    step_weight,
    mixer_conv,
    mixer_shift,
    state_conv,
    state_shift,
    step_bias,
    decay_log,
    skip_gain,
    gate_gain,
    out_weight,
    out_grad,
):
    length, width = block_input.shape
    inner = gate_weight.shape[1]
    heads_local = step_weight.shape[1]
    groups = lax.axis_size("tensor")
    member = lax.axis_index("tensor")
    columns = width // groups
    total_inner = inner * groups

    gain, marks, chan, state_chan, heads, small_weight = prepare(
        length,
        width,
        inner,
        (
            segment_ids,
            norm_gain,
            mixer_conv,
            mixer_shift,
            state_conv,
            state_shift,
            step_bias,
            decay_log,
            skip_gain,
            gate_gain,
            state_weight,
            step_weight,
        ),
    )
    params = (
        gain,
        gate_weight,
        input_weight,
        small_weight,
        chan,
        state_chan,
        heads,
        out_weight,
    )
    blocks = length // ROWS
    line = Line(groups, member)
    saved, carry, after = None, [], []
    block_sums, waiting = [], []
    for block in range(blocks):
        early = block < blocks // 2
        saved, partial, sums, carry = forward(
            block,
            segment_ids,
            marks,
            block_input,
            out_grad,
            params,
            carry,
            saved,
            after,
            early,
        )
        block_sums.append(sums)
        after = [partial]
        if early:
            line.push(partial, "output", block * ROWS)
        else:
            waiting.append(partial)
        if block == blocks // 2:
            after = line.tick({}, after)
    sums = jnp.concatenate(block_sums, axis=1)
    after = line.tick({}, [sums])
    sums = sum_over(sums, "tensor", groups)
    partials = project_rows(waiting, out_weight, [*after, sums])
    ending = {
        "output": (block_input, sums, total_inner),
        "input": (out_grad, sums, 0),
    }
    for k, partial in enumerate(partials):
        line.push(partial, "output", (blocks // 2 + k) * ROWS)
    after = [partials[0]]
    normed, *saved = saved
    grad_low, gate_low, gate_out, gate_sums = gate_grads(
        total_inner, sums, saved[7], saved[0], saved[8], chan, after
    )
    (gate_weight_grad,) = weight_grads(normed, [gate_low], [grad_low])
    (out_weight_grad,) = weight_grads(gate_out, [out_grad], [gate_weight_grad])
    after = [out_weight_grad]
    gate_weight_grad, out_weight_grad = lax.psum((gate_weight_grad, out_weight_grad), "dp")
    after = line.tick(ending, after)
    lows, carry = None, []
    for block in reversed(range(blocks)):
        lows, partials, carry = backward(
            block,
            segment_ids,
            marks,
            block_input,
            params,
            saved,
            (grad_low, gate_low),
            carry,
            lows,
            after + [gate_weight_grad, out_weight_grad] if block == blocks // 2 - 1 else after,
            2 if block == 0 else 1,
        )
        after = [partials[0]]
        for k, partial in enumerate(partials):
            line.push(partial, "input", block * ROWS + k * partial.shape[0])
        if block > 0:
            after = line.tick(ending, after)
    mixer_low, small_low = lows
    chan_sums, state_sums, head_sums, gain_sums = carry[2:]
    weight_sums = weight_grads(
        normed,
        [mixer_low, small_low],
        after,
        (chan_sums, gate_sums, head_sums, state_sums, gain_sums),
    )
    after = [weight_sums[0]]
    input_weight_grad, state_weight_grad, packed = lax.psum(tuple(weight_sums), "dp")
    after = line.tick(ending, after, first=2)
    ticks = 0
    while line.busy():
        after = after + [input_weight_grad] if ticks == 1 else after
        if line.pending() == 1:
            line_sums, state_weight_grad = sum_pieces(
                packed, state_weight_grad, "tensor", groups, member, after
            )
        after = line.tick(ending, after, first=2)
        ticks += 1
    block_output = line.outs["output"]
    input_grad = line.outs["input"]
    packed = packed.astype(f32)
    return (
        block_output,
        input_grad,
        lax.dynamic_slice_in_dim(line_sums[:, 13].reshape(-1), member * columns, columns, 0),
        gate_weight_grad.astype(f32),
        input_weight_grad.astype(f32),
        state_weight_grad,
        packed[16 : 16 + heads_local].T,
        packed[1:5, :inner],
        packed[5, :inner],
        line_sums[0, 8:12],
        line_sums[0, 12],
        packed[7, :heads_local],
        packed[7, LANES : LANES + heads_local],
        packed[0, :inner].reshape(heads_local, inner // heads_local).sum(axis=1),
        packed[6, :inner],
        out_weight_grad.astype(f32),
    )


def solution(mesh):
    return jax.shard_map(
        on_device,
        mesh=mesh,
        in_specs=(
            P("dp", None),
            P("dp"),
            P(),
            P(None, "tensor"),
            P(None, "tensor"),
            P(),
            P(None, "tensor"),
            P(None, "tensor"),
            P("tensor"),
            P(),
            P(),
            P("tensor"),
            P("tensor"),
            P("tensor"),
            P("tensor"),
            P("tensor", None),
            P("dp", None),
        ),
        out_specs=(
            P("dp", None),
            P("dp", None),
            P("tensor"),
            P(None, "tensor"),
            P(None, "tensor"),
            P("tensor", None),
            P(None, "tensor"),
            P(None, "tensor"),
            P("tensor"),
            P(),
            P(),
            P("tensor"),
            P("tensor"),
            P("tensor"),
            P("tensor"),
            P("tensor", None),
        ),
        check_vma=False,
    )
```

time: 1960 us -> 515 us (0.26)
  waiting for transfers between devices: 945 us -> 86.2 us
  matrix products: 698 us -> 0 us
  Pallas kernels: 0 us -> 297 us
  other arithmetic: 133 us -> 9.89 us
  local copies, waits for them, and re-layouts: 111 us -> 18.5 us
  starting transfers between devices: 0.12 us -> 81.6 us
  blocking collectives: 48.2 us -> 0 us
    psum x3 -> x2, waiting for transfers between devices: 945 us -> 7.16 us  [the longest x1 7.14 us: on_device(): lax.psum(tuple(weight_sums), 'dp')]
    dot_general x54 -> x0, matrix products: 698 us -> none  [the longest x18 311 us: against_rows(): lax.dot_general(left, right, (((1,), (1,)), ((), ())), preferred_element_...]
    pallas_call x0 -> x43, Pallas kernels: none -> 297 us  [the longest x4 86.6 us: backward(): pl.pallas_call(functools.partial(backward_kernel, block=block, first=not...]
    ppermute x0 -> x33, starting transfers between devices: none -> 81.5 us  [the longest x27 72.8 us: launch(): moved = lax.ppermute(total, 'tensor', self.steps[step][1])]
    ppermute x0 -> x33, waiting for transfers between devices: none -> 79 us  [the longest x27 61.7 us: launch(): moved = lax.ppermute(total, 'tensor', self.steps[step][1])]
    reduce_sum x8 -> x1, other arithmetic: 52.6 us -> 0.63 us  [on_device(): packed[0, :inner].reshape(heads_local, inner // heads_local).sum(axis=1)]
    psum x3 -> x0, blocking collectives: 48.2 us -> none  [the longest x1 26.1 us: on_device(): lax.psum((norm_gain_grad, gate_weight_grad, input_weight_grad, state_weig...]
    dynamic_update_slice x24 -> x0, local copies, waits for them, and re-layouts: 35.9 us -> none  [on_device(): lax.scan(backward_head, jnp.zeros((length, length), jnp.float32), (head_v...]
  transfers between devices with their start and end apart: 3 -> 35, of which waited for: 2 -> 9; matrix products, arithmetic and copies ran while one was open for 8% -> 4% of each run, Pallas kernels for 0% -> 52%
where the time goes in v1:
time: 515 us; the launch traced here: 508 us
  Pallas kernels  297 us (58%)
  waiting for transfers between devices  86.2 us (17%)
  starting transfers between devices  81.6 us (16%)
  local copies, waits for them, and re-layouts  18.5 us (4%)
  between operations  15 us (3%)
  other arithmetic  9.89 us (2%)
    pallas_call x4, Pallas kernels, backward(): pl.pallas_call(functools.partial(backward_kernel, block=block, first=not...  86.6 us
    ppermute x27, starting transfers between devices, launch(): moved = lax.ppermute(total, 'tensor', self.steps[step][1])  72.8 us
    pallas_call x4, Pallas kernels, forward(): pl.pallas_call(functools.partial(forward_kernel, block=block, first=not c...  72.8 us
    ppermute x27, waiting for transfers between devices, launch(): moved = lax.ppermute(total, 'tensor', self.steps[step][1])  61.7 us
    pallas_call x18, Pallas kernels, land(): pl.pallas_call(functools.partial(land_kernel, mode=mode, unread=len(after...  47.7 us
    pallas_call x3, Pallas kernels, weight_grads(): pl.pallas_call(functools.partial(weight_kernel, rights=len(rights), unrea...  33.6 us
    pallas_call x9, Pallas kernels, finish(): pl.pallas_call(functools.partial(finish_kernel, adds=adds, inner=inner, r...  31.4 us
    pallas_call x1, Pallas kernels, gate_grads(): pl.pallas_call(functools.partial(gate_kernel, total_inner, unread=len(aft...  11.6 us
  transfers between devices with their start and end apart: 35, of which 9 were waited for; matrix products, arithmetic and copies ran while one was open for 4% of the time, Pallas kernels for 52%

profile of v1, /device:TPU:0, one launch (start us, length us, event | category | flops | bytes accessed | tf_op | source)
XLA Modules:
  0.0 507.8 jit_solution(7326848729695490210)
XLA Ops:
  8.9 2.8 prepare.1
  11.7 18.1 %forward_mix.4 = (bf16[2048,1536]{1,0:T(8,128)(2,1)}, bf16[2048,768]{1,0:T(8,128)(2,1)}, bf16[2048,768]{1,0:T(8,128)(2,1)}, bf16[2048,384]{1,0:T(8,128)(2,1)}, b...) custom-call(s32[2048]{0:T(1024)} %starts.15, ...), custom_call_target="tpu_custom_call" | custom-call | flops 1000 | bytes 1000 | tf_op jit(solution)/shard_map/forward_mix/pallas_call | solution.py:469
  29.8 5.3 %collective-permute-start = (bf16[512,1536]{1,0:T(8,128)(2,1)}, bf16[512,1536]{1,0:T(8,128)(2,1)S(1)}, u32[]{:S(2)}, u32[]{:S(2)}) collective-permute-start(bf16[512,1536]{1,0:T(8,128)(2,1)} %get-tuple-element.149.rest_13_.total_home), channel_id=1, source_target_pairs={{0,1},{3,2},{4,5},{7,6},{8,9},{11,10},{12,13},{15,14},{16,17},{19,... | collective-permute-start | bytes 4718600 | tf_op jit(solution)/shard_map/ppermute | solution.py:1192
  35.2 18.4 %forward_mix.5 = (bf16[2048,1536]{1,0:T(8,128)(2,1)}, bf16[2048,768]{1,0:T(8,128)(2,1)}, bf16[2048,768]{1,0:T(8,128)(2,1)}, bf16[2048,384]{1,0:T(8,128)(2,1)}, b...) custom-call(s32[2048]{0:T(1024)} %starts.15, ...), custom_call_target="tpu_custom_call", output_to_operand_aliasing={{0}: (14, {}), {1}: (15, {}), {2}: (16, {}), {3}: (17, {}),... | custom-call | flops 1000 | bytes 1000 | tf_op jit(solution)/shard_map/forward_mix/pallas_call | solution.py:469
  55.0 18.1 %forward_mix.6 = (bf16[2048,1536]{1,0:T(8,128)(2,1)}, bf16[2048,768]{1,0:T(8,128)(2,1)}, bf16[2048,768]{1,0:T(8,128)(2,1)}, bf16[2048,384]{1,0:T(8,128)(2,1)}, b...) custom-call(s32[2048]{0:T(1024)} %starts.15, ...), custom_call_target="tpu_custom_call", output_to_operand_aliasing={{0}: (14, {}), {1}: (15, {}), {2}: (16, {}), {3}: (17, {}),... | custom-call | flops 1000 | bytes 1000 | tf_op jit(solution)/shard_map/forward_mix/pallas_call | solution.py:469
  74.3 2.7 line_land.18.rest_13_.total_home
  78.4 18.2 %forward_mix.7 = (bf16[2048,1536]{1,0:T(8,128)(2,1)}, bf16[2048,768]{1,0:T(8,128)(2,1)}, bf16[2048,768]{1,0:T(8,128)(2,1)}, bf16[2048,384]{1,0:T(8,128)(2,1)}, b...) custom-call(s32[2048]{0:T(1024)} %starts.15, ...), custom_call_target="tpu_custom_call", output_to_operand_aliasing={{0}: (14, {}), {1}: (15, {}), {2}: (16, {}), {3}: (17, {}),... | custom-call | flops 1000 | bytes 1000 | tf_op jit(solution)/shard_map/forward_mix/pallas_call | solution.py:469
  99.1 2.5 collective-permute-start.5
  104.2 2.7 line_land.19.rest_0_.total_home
  106.9 8.2 %collective-permute-done.4 = f32[2,2048]{1,0:T(2,128)S(1)} collective-permute-done((f32[2,2048]{1,0:T(2,128)S(1)}, f32[2,2048]{1,0:T(2,128)S(1)}, u32[]{:S(2)}, u32[]{:S(2)}) %collective-permute-start.4) | collective-permute-done | bytes 16416 | tf_op jit(solution)/shard_map/ppermute | solution.py:1235
  117.7 2.7 line_land.20.refs_3_.total_home
  120.5 5.8 %project_rows.1 = (bf16[512,1536]{1,0:T(8,128)(2,1)}, bf16[512,1536]{1,0:T(8,128)(2,1)}) custom-call(bf16[512,768]{1,0:T(8,128)(2,1)} %get-tuple-element.164.rest_0_.refs_0_, bf16[512,768]{1,0:T(8,128)(2,1)} %get-tuple-element.178.refs_1_, bf16[768,1536]{1,0:T(8,128)(2,1)} %refs_2_.1, bf16[512,1536]{1,0:T(8,128)(2,1)} %line_land.20.refs_3_.total_home, ...), custom_call_target="tpu_custom_call" | custom-call | flops 1000 | bytes 1000 | tf_op jit(solution)/shard_map/project_rows/pallas_call | solution.py:516
  126.2 3.8 collective-permute-start.9
  133.1 6.9 %collective-permute-start.6 = (bf16[512,1536]{1,0:T(8,128)(2,1)}, bf16[512,1536]{1,0:T(8,128)(2,1)}, u32[]{:S(2)}, u32[]{:S(2)}) collective-permute-start(bf16[512,1536]{1,0:T(8,128)(2,1)} %get-tuple-element.183.total_home), channel_id=1, source_target_pairs={{0,1},{3,2},{4,5},{7,6},{8,9},{11,10},{12,13},{15,14},{16,17},{19,... | collective-permute-start | bytes 4718600 | tf_op jit(solution)/shard_map/ppermute | solution.py:1192
  140.0 11.6 %gate_grads.1 = (bf16[2048,768]{1,0:T(8,128)(2,1)}, bf16[2048,768]{1,0:T(8,128)(2,1)}, bf16[2048,768]{1,0:T(8,128)(2,1)}, f32[8,768]{1,0:T(8,128)}) custom-call(f32[2,2048]{1,0:T(2,128)} %add_add_fusion.refs_4_.sums, f32[2048,768]{1,0:T(8,128)} %get-tuple-element.184.mixed.rest_0_, bf16[2048,768]{1,0:T(8,128)(2,1)} %get-tuple-element.185.gate_raw, ...), custom_call_target="tpu_custom_call" | custom-call | flops 1000 | bytes 1000 | tf_op jit(solution)/shard_map/gate_grads/pallas_call | solution.py:574
  151.6 9.5 %weight_grads.3.rest_1_ = bf16[1536,768]{1,0:T(8,128)(2,1)} custom-call(bf16[2048,1536]{1,0:T(8,128)(2,1)} %get-tuple-element.198.left, bf16[2048,768]{1,0:T(8,128)(2,1)} %get-tuple-element.196.rest_0_.rest_9_, bf16[2048,768]{1,0:T(8,128)(2,1)} %get-tuple-element.188.rest_1_), custom_call_target="tpu_custom_call" | custom-call | flops 1000 | bytes 1000 | tf_op jit(solution)/shard_map/weight_grads/pallas_call | solution.py:1015
  161.1 9.5 %weight_grads.4.rest_0_ = bf16[768,1536]{1,0:T(8,128)(2,1)} custom-call(bf16[2048,768]{1,0:T(8,128)(2,1)} %get-tuple-element.197.left, bf16[2048,1536]{1,0:T(8,128)(2,1)} %base_home.17, bf16[1536,768]{1,0:T(8,128)(2,1)} %weight_grads.3.rest_1_), custom_call_target="tpu_custom_call" | custom-call | flops 1000 | bytes 1000 | tf_op jit(solution)/shard_map/weight_grads/pallas_call | solution.py:1015
  170.6 2.7 line_land.21.rest_0_.total_home
  175.2 2.7 line_land.22.rest_0_.total_home
  179.3 3.7 line_finish.9.rest_14_.rest_0_
  183.0 21.4 %backward_mix.4 = (bf16[2048,768]{1,0:T(8,128)(2,1)}, bf16[2048,384]{1,0:T(8,128)(2,1)}, bf16[512,1536]{1,0:T(8,128)(2,1)}, f32[128,768]{1,0:T(8,128)}, f32[8,10...) custom-call(s32[2048]{0:T(1024)} %starts.15, ...), custom_call_target="tpu_custom_call" | custom-call | flops 1000 | bytes 1000 | tf_op jit(solution)/shard_map/backward_mix/pallas_call | solution.py:914
  204.4 7.8 %collective-permute-start.11 = (bf16[512,1536]{1,0:T(8,128)(2,1)}, bf16[512,1536]{1,0:T(8,128)(2,1)}, u32[]{:S(2)}, u32[]{:S(2)}) collective-permute-start(bf16[512,1536]{1,0:T(8,128)(2,1)} %get-tuple-element.199.rest_0_.total_home), channel_id=1, source_target_pairs={{0,1},{3,2},{4,5},{7,6},{8,9},{11,10},{12,13},{15,14},{16,17},{19,... | collective-permute-start | bytes 4718600 | tf_op jit(solution)/shard_map/ppermute | solution.py:1192
  212.3 2.7 line_land.23.rest_0_.total_home
  216.8 2.8 line_land.24.rest_1_.total_home
  221.0 3.8 line_finish.10.rest_22_.rest_0_
  224.7 21.9 %backward_mix.5 = (bf16[2048,768]{1,0:T(8,128)(2,1)}, bf16[2048,384]{1,0:T(8,128)(2,1)}, bf16[512,1536]{1,0:T(8,128)(2,1)}, f32[128,768]{1,0:T(8,128)}, f32[8,10...) custom-call(s32[2048]{0:T(1024)} %starts.15, ...), custom_call_target="tpu_custom_call", output_to_operand_aliasing={{0}: (26, {}), {1}: (27, {})} | custom-call | flops 1000 | bytes 1000 | tf_op jit(solution)/shard_map/backward_mix/pallas_call | solution.py:914
  246.6 4.8 collective-permute-start.17
  251.4 2.8 line_land.25.rest_0_.total_home
  256.1 2.8 line_land.26.rest_1_.total_home
  261.3 3.6 line_finish.11.rest_22_.rest_0_
  264.9 21.6 %backward_mix.6 = (bf16[2048,768]{1,0:T(8,128)(2,1)}, bf16[2048,384]{1,0:T(8,128)(2,1)}, bf16[512,1536]{1,0:T(8,128)(2,1)}, f32[128,768]{1,0:T(8,128)}, f32[8,10...) custom-call(s32[2048]{0:T(1024)} %starts.15, ...), custom_call_target="tpu_custom_call", output_to_operand_aliasing={{0}: (26, {}), {1}: (27, {})} | custom-call | flops 1000 | bytes 1000 | tf_op jit(solution)/shard_map/backward_mix/pallas_call | solution.py:914
  286.5 6.9 %collective-permute-start.22 = (bf16[512,1536]{1,0:T(8,128)(2,1)}, bf16[512,1536]{1,0:T(8,128)(2,1)}, u32[]{:S(2)}, u32[]{:S(2)}) collective-permute-start(bf16[512,1536]{1,0:T(8,128)(2,1)} %get-tuple-element.217.rest_0_.total_home), channel_id=1, source_target_pairs={{0,1},{3,2},{4,5},{7,6},{8,9},{11,10},{12,13},{15,14},{16,17},{19,... | collective-permute-start | bytes 4718600 | tf_op jit(solution)/shard_map/ppermute | solution.py:1192
  294.5 2.8 line_land.27.rest_0_.total_home
  297.3 2.3 collective-permute-start.20
  299.6 2.7 line_land.28.rest_1_.total_home
  303.6 3.6 line_finish.12.rest_22_
  307.2 21.6 %backward_mix.7 = (bf16[2048,768]{1,0:T(8,128)(2,1)}, bf16[2048,384]{1,0:T(8,128)(2,1)}, bf16[256,1536]{1,0:T(8,128)(2,1)}, bf16[256,1536]{1,0:T(8,128)(2,1)}, f...) custom-call(s32[2048]{0:T(1024)} %starts.15, ...), custom_call_target="tpu_custom_call", output_to_operand_aliasing={{0}: (26, {}), {1}: (27, {})} | custom-call | flops 1000 | bytes 1000 | tf_op jit(solution)/shard_map/backward_mix/pallas_call | solution.py:914
  328.8 14.6 %weight_grads.5 = (bf16[1536,768]{1,0:T(8,128)(2,1)}, bf16[1536,256]{1,0:T(8,128)(2,1)}, bf16[32,1536]{1,0:T(8,128)(2,1)}) custom-call(bf16[2048,1536]{1,0:T(8,128)(2,1)} %get-tuple-element.198.left, bf16[2048,768]{1,0:T(8,128)(2,1)} %get-tuple-element.228.rest_0_, bf16[2048,384]{1,0:T(8,128)(2,1)} %get-tuple-element.229.rest_1_, ...), custom_call_target="tpu_custom_call" | custom-call | flops 1000 | bytes 1000 | tf_op jit(solution)/shard_map/weight_grads/pallas_call | solution.py:1015
  343.4 2.8 line_land.29.rest_0_.total_home
  348.1 7.3 %collective-permute-start.21 = (bf16[256,1536]{1,0:T(8,128)(2,1)S(1)}, bf16[256,1536]{1,0:T(8,128)(2,1)}, u32[]{:S(2)}, u32[]{:S(2)}) collective-permute-start(bf16[256,1536]{1,0:T(8,128)(2,1)S(1)} %copy-done.7), channel_id=1, source_target_pairs={{0,1},{3,2},{4,5},{7,6},{8,9},{11,10},{12,13},{15,14},{16,17},{19,... | collective-permute-start | bytes 2359304 | tf_op jit(solution)/shard_map/ppermute | solution.py:1192
  355.4 2.2 collective-permute-start.18
  357.6 14.9 %collective-permute-done.21.moved_home = bf16[256,1536]{1,0:T(8,128)(2,1)} collective-permute-done((bf16[256,1536]{1,0:T(8,128)(2,1)S(1)}, bf16[256,1536]{1,0:T(8,128)(2,1)}, u32[]{:S(2)}, u32[]{:S(2)}) %collective-permute-start.21) | collective-permute-done | bytes 786464 | tf_op jit(solution)/shard_map/ppermute | solution.py:1192
  372.4 2.2 line_land.30.rest_0_.total_home
  374.7 2.8 line_land.31.rest_0_.total_home
  379.9 3.7 line_finish.13.rest_0_
  384.5 2.2 line_land.32.rest_0_.total_home
  386.8 2.9 line_land.33.rest_1_.total_home
  393.3 23.7 %collective-permute-done.26.moved_home = bf16[512,1536]{1,0:T(8,128)(2,1)} collective-permute-done((bf16[512,1536]{1,0:T(8,128)(2,1)}, bf16[512,1536]{1,0:T(8,128)(2,1)}, u32[]{:S(2)}, u32[]{:S(2)}) %collective-permute-start.26) | collective-permute-done | bytes 1572896 | tf_op jit(solution)/shard_map/ppermute | solution.py:1192
  417.0 3.6 line_finish.14.rest_0_
  420.6 7.1 %all-reduce.5.cloned.1.call-done = (bf16[1536,768]{1,0:T(8,128)(2,1)}, bf16[32,1536]{1,0:T(8,128)(2,1)}, bf16[1536,256]{1,0:T(8,128)(2,1)}) async-done(((bf16[1536,768]{1,0:T(8,128)(2,1)}, bf16[32,1536]{1,0:T(8,128)(2,1)}, bf16[1536,256]{1,0:T(8,128)(2,1)}), (bf16[1536,768]{1,0:T(8,128)(2,1)}, bf16[32,1536]{1,0:T(8,128)(2,1)}, bf16[1536,256]{1,0:T(8,128)(2,1)})) %all-reduce.5.cloned.1.call-update) | async-done | bytes 3244048 | tf_op jit(solution)/shard_map/psum | solution.py:1425
  427.8 2.3 line_land.34.rest_1_.total_home
  431.5 2.5 convert_element_type.15
  434.0 2.8 convert_element_type.18
  436.9 9.2 %collective-permute-done.25.moved_home = bf16[512,1536]{1,0:T(8,128)(2,1)} collective-permute-done((bf16[512,1536]{1,0:T(8,128)(2,1)}, bf16[512,1536]{1,0:T(8,128)(2,1)}, u32[]{:S(2)}, u32[]{:S(2)}) %collective-permute-start.25) | collective-permute-done | bytes 1572896 | tf_op jit(solution)/shard_map/ppermute | solution.py:1192
  446.0 3.5 line_finish.15.rest_0_
  449.6 2.2 line_land.35.rest_1_.total_home
  453.8 11.5 %collective-permute-done.29.moved_home = bf16[256,1536]{1,0:T(8,128)(2,1)} collective-permute-done((bf16[256,1536]{1,0:T(8,128)(2,1)}, bf16[256,1536]{1,0:T(8,128)(2,1)}, u32[]{:S(2)}, u32[]{:S(2)}) %collective-permute-start.29) | collective-permute-done | bytes 786464 | tf_op jit(solution)/shard_map/ppermute | solution.py:1192
  465.3 3.0 line_finish.16.rest_0_
  468.3 2.3 part_pieces.1
  470.6 4.4 collective-permute-start.32
  475.6 2.5 convert_element_type.16
  480.7 9.1 %collective-permute-done.30.refs_1_ = bf16[480,256]{1,0:T(8,128)(2,1)S(1)} collective-permute-done((bf16[480,256]{1,0:T(8,128)(2,1)}, bf16[480,256]{1,0:T(8,128)(2,1)S(1)}, u32[]{:S(2)}, u32[]{:S(2)}) %collective-permute-start.30) | collective-permute-done | bytes 245792 | tf_op jit(solution)/shard_map/ppermute | solution.py:1277
  490.6 2.2 join_pieces.1
  497.7 3.0 line_finish.17
  (120 shorter events, 50.5 us)
Async XLA Ops:
  29.8 43.2 %collective-permute-start = (bf16[512,1536]{1,0:T(8,128)(2,1)}, bf16[512,1536]{1,0:T(8,128)(2,1)S(1)}, u32[]{:S(2)}, u32[]{:S(2)}) collective-permute-start(bf16[512,1536]{1,0:T(8,128)(2,1)} %get-tuple-element.149.rest_13_.total_home), channel_id=1, source_target_pairs={{0,1},{3,2},{4,5},{7,6},{8,9},{11,10},{12,13},{15,14},{16,17},{19,... | collective-permute-start | bytes 4718600 | tf_op jit(solution)/shard_map/ppermute | solution.py:1192
  53.6 49.4 %collective-permute-start.2 = (bf16[512,1536]{1,0:T(8,128)(2,1)}, bf16[512,1536]{1,0:T(8,128)(2,1)S(1)}, u32[]{:S(2)}, u32[]{:S(2)}) collective-permute-start(bf16[512,1536]{1,0:T(8,128)(2,1)} %get-tuple-element.163.rest_13_.total_home), channel_id=1, source_target_pairs={{0,1},{3,2},{4,5},{7,6},{8,9},{11,10},{12,13},{15,14},{16,17},{19,... | collective-permute-start | bytes 4718600 | tf_op jit(solution)/shard_map/ppermute | solution.py:1192
  73.1 1.2 copy-start.12
  74.3 4.1 copy-start.21
  74.3 4.1 copy-start.22
  74.3 4.1 copy-start.23
  77.1 39.4 %collective-permute-start.1 = (bf16[512,1536]{1,0:T(8,128)(2,1)}, bf16[512,1536]{1,0:T(8,128)(2,1)S(1)}, u32[]{:S(2)}, u32[]{:S(2)}) collective-permute-start(bf16[512,1536]{1,0:T(8,128)(2,1)} %line_land.18.rest_13_.total_home), channel_id=1, source_target_pairs={{1,2},{2,1},{5,6},{6,5},{9,10},{10,9},{13,14},{14,13},{17,18},{18,... | collective-permute-start | bytes 4718600 | tf_op jit(solution)/shard_map/ppermute | solution.py:1192
  97.3 5.7 %copy-start.20 = (f32[2,2048]{1,0:T(2,128)}, f32[2,2048]{1,0:T(2,128)S(1)}, u32[]{:S(2)}) copy-start(f32[2,2048]{1,0:T(2,128)S(1)} %constant_dynamic-update-slice_fusion.rest_0_) | copy-start | bytes 49156
  97.3 17.9 %collective-permute-start.4 = (f32[2,2048]{1,0:T(2,128)S(1)}, f32[2,2048]{1,0:T(2,128)S(1)}, u32[]{:S(2)}, u32[]{:S(2)}) collective-permute-start(f32[2,2048]{1,0:T(2,128)S(1)} %constant_dynamic-update-slice_fusion.rest_0_), channel_id=1, source_target_pairs={{0,2},{1,3},{2,0},{3,1},{4,6},{5,7},{6,4},{7,5},{8,10},{9,11},{10,... | collective-permute-start | bytes 49160 | tf_op jit(solution)/shard_map/ppermute | solution.py:1235
  99.1 16.1 %collective-permute-start.5 = (f32[2,2048]{1,0:T(2,128)S(1)}, f32[2,2048]{1,0:T(2,128)S(1)}, u32[]{:S(2)}, u32[]{:S(2)}) collective-permute-start(f32[2,2048]{1,0:T(2,128)S(1)} %constant_dynamic-update-slice_fusion.rest_0_), channel_id=1, source_target_pairs={{0,3},{1,2},{2,1},{3,0},{4,7},{5,6},{6,5},{7,4},{8,11},{9,10},{10,... | collective-permute-start | bytes 49160 | tf_op jit(solution)/shard_map/ppermute | solution.py:1235
  101.6 13.6 %collective-permute-start.3 = (f32[2,2048]{1,0:T(2,128)S(1)}, f32[2,2048]{1,0:T(2,128)S(1)}, u32[]{:S(2)}, u32[]{:S(2)}) collective-permute-start(f32[2,2048]{1,0:T(2,128)S(1)} %constant_dynamic-update-slice_fusion.rest_0_), channel_id=1, source_target_pairs={{0,1},{1,0},{2,3},{3,2},{4,5},{5,4},{6,7},{7,6},{8,9},{9,8},{10,11... | collective-permute-start | bytes 49160 | tf_op jit(solution)/shard_map/ppermute | solution.py:1235
  103.0 1.2 copy-start.8
  116.5 1.2 copy-start.11
  120.4 9.6 %copy-start = (bf16[512,1536]{1,0:T(8,128)(2,1)S(1)}, bf16[512,1536]{1,0:T(8,128)(2,1)}, u32[]{:S(2)}) copy-start(bf16[512,1536]{1,0:T(8,128)(2,1)} %line_land.19.rest_0_.total_home) | copy-start | bytes 4718596
  120.4 11.4 %copy-start.1 = (bf16[512,1536]{1,0:T(8,128)(2,1)S(1)}, bf16[512,1536]{1,0:T(8,128)(2,1)}, u32[]{:S(2)}) copy-start(bf16[512,1536]{1,0:T(8,128)(2,1)} %line_land.20.refs_3_.total_home) | copy-start | bytes 4718596
  126.2 44.4 %collective-permute-start.9 = (bf16[512,1536]{1,0:T(8,128)(2,1)}, bf16[512,1536]{1,0:T(8,128)(2,1)}, u32[]{:S(2)}, u32[]{:S(2)}) collective-permute-start(bf16[512,1536]{1,0:T(8,128)(2,1)} %get-tuple-element.187.rest_0_.total_home), channel_id=1, source_target_pairs={{0,1},{3,2},{4,5},{7,6},{8,9},{11,10},{12,13},{15,14},{16,17},{19,... | collective-permute-start | bytes 4718600 | tf_op jit(solution)/shard_map/ppermute | solution.py:1192
  130.0 45.2 %collective-permute-start.8 = (bf16[512,1536]{1,0:T(8,128)(2,1)S(1)}, bf16[512,1536]{1,0:T(8,128)(2,1)}, u32[]{:S(2)}, u32[]{:S(2)}) collective-permute-start(bf16[512,1536]{1,0:T(8,128)(2,1)S(1)} %copy-done), channel_id=1, source_target_pairs={{1,2},{2,1},{5,6},{6,5},{9,10},{10,9},{13,14},{14,13},{17,18},{18,... | collective-permute-start | bytes 4718600 | tf_op jit(solution)/shard_map/ppermute | solution.py:1192
  131.8 47.5 %collective-permute-start.7 = (bf16[512,1536]{1,0:T(8,128)(2,1)S(1)}, bf16[512,1536]{1,0:T(8,128)(2,1)}, u32[]{:S(2)}, u32[]{:S(2)}) collective-permute-start(bf16[512,1536]{1,0:T(8,128)(2,1)S(1)} %copy-done.1), channel_id=1, source_target_pairs={{1,0},{2,3},{5,4},{6,7},{9,8},{10,11},{13,12},{14,15},{17,16},{18,... | collective-permute-start | bytes 4718600 | tf_op jit(solution)/shard_map/ppermute | solution.py:1192
  133.1 79.2 %collective-permute-start.6 = (bf16[512,1536]{1,0:T(8,128)(2,1)}, bf16[512,1536]{1,0:T(8,128)(2,1)}, u32[]{:S(2)}, u32[]{:S(2)}) collective-permute-start(bf16[512,1536]{1,0:T(8,128)(2,1)} %get-tuple-element.183.total_home), channel_id=1, source_target_pairs={{0,1},{3,2},{4,5},{7,6},{8,9},{11,10},{12,13},{15,14},{16,17},{19,... | collective-permute-start | bytes 4718600 | tf_op jit(solution)/shard_map/ppermute | solution.py:1192
  173.3 91.5 %all-reduce.7.cloned.1.call-start = ((), (), s32[]{:S(2)}) async-start(), calls=%async_computation.1 | async-start | bytes 9437184 | tf_op jit(solution)/shard_map/psum | solution.py:1394
  173.4 43.4 %collective-permute-start.13 = (bf16[512,1536]{1,0:T(8,128)(2,1)}, bf16[512,1536]{1,0:T(8,128)(2,1)}, u32[]{:S(2)}, u32[]{:S(2)}) collective-permute-start(bf16[512,1536]{1,0:T(8,128)(2,1)} %line_land.21.rest_0_.total_home), channel_id=1, source_target_pairs={{1,2},{2,1},{5,6},{6,5},{9,10},{10,9},{13,14},{14,13},{17,18},{18,... | collective-permute-start | bytes 4718600 | tf_op jit(solution)/shard_map/ppermute | solution.py:1192
  178.0 43.0 %collective-permute-start.12 = (bf16[512,1536]{1,0:T(8,128)(2,1)}, bf16[512,1536]{1,0:T(8,128)(2,1)}, u32[]{:S(2)}, u32[]{:S(2)}) collective-permute-start(bf16[512,1536]{1,0:T(8,128)(2,1)} %line_land.22.rest_0_.total_home), channel_id=1, source_target_pairs={{1,0},{2,3},{5,4},{6,7},{9,8},{10,11},{13,12},{14,15},{17,16},{18,... | collective-permute-start | bytes 4718600 | tf_op jit(solution)/shard_map/ppermute | solution.py:1192
  204.4 47.0 %collective-permute-start.11 = (bf16[512,1536]{1,0:T(8,128)(2,1)}, bf16[512,1536]{1,0:T(8,128)(2,1)}, u32[]{:S(2)}, u32[]{:S(2)}) collective-permute-start(bf16[512,1536]{1,0:T(8,128)(2,1)} %get-tuple-element.199.rest_0_.total_home), channel_id=1, source_target_pairs={{0,1},{3,2},{4,5},{7,6},{8,9},{11,10},{12,13},{15,14},{16,17},{19,... | collective-permute-start | bytes 4718600 | tf_op jit(solution)/shard_map/ppermute | solution.py:1192
  215.0 41.1 %collective-permute-start.10 = (bf16[512,1536]{1,0:T(8,128)(2,1)}, bf16[512,1536]{1,0:T(8,128)(2,1)}, u32[]{:S(2)}, u32[]{:S(2)}) collective-permute-start(bf16[512,1536]{1,0:T(8,128)(2,1)} %line_land.23.rest_0_.total_home), channel_id=1, source_target_pairs={{1,2},{2,1},{5,6},{6,5},{9,10},{10,9},{13,14},{14,13},{17,18},{18,... | collective-permute-start | bytes 4718600 | tf_op jit(solution)/shard_map/ppermute | solution.py:1192
  219.6 40.5 %collective-permute-start.15 = (bf16[512,1536]{1,0:T(8,128)(2,1)}, bf16[512,1536]{1,0:T(8,128)(2,1)S(1)}, u32[]{:S(2)}, u32[]{:S(2)}) collective-permute-start(bf16[512,1536]{1,0:T(8,128)(2,1)} %line_land.24.rest_1_.total_home), channel_id=1, source_target_pairs={{1,0},{2,3},{5,4},{6,7},{9,8},{10,11},{13,12},{14,15},{17,16},{18,... | collective-permute-start | bytes 4718600 | tf_op jit(solution)/shard_map/ppermute | solution.py:1192
  246.6 46.7 %collective-permute-start.17 = (bf16[512,1536]{1,0:T(8,128)(2,1)}, bf16[512,1536]{1,0:T(8,128)(2,1)S(1)}, u32[]{:S(2)}, u32[]{:S(2)}) collective-permute-start(bf16[512,1536]{1,0:T(8,128)(2,1)} %get-tuple-element.208.rest_0_.total_home), channel_id=1, source_target_pairs={{0,1},{3,2},{4,5},{7,6},{8,9},{11,10},{12,13},{15,14},{16,17},{19,... | collective-permute-start | bytes 4718600 | tf_op jit(solution)/shard_map/ppermute | solution.py:1192
  254.2 45.3 %collective-permute-start.16 = (bf16[512,1536]{1,0:T(8,128)(2,1)}, bf16[512,1536]{1,0:T(8,128)(2,1)}, u32[]{:S(2)}, u32[]{:S(2)}) collective-permute-start(bf16[512,1536]{1,0:T(8,128)(2,1)} %line_land.25.rest_0_.total_home), channel_id=1, source_target_pairs={{1,2},{2,1},{5,6},{6,5},{9,10},{10,9},{13,14},{14,13},{17,18},{18,... | collective-permute-start | bytes 4718600 | tf_op jit(solution)/shard_map/ppermute | solution.py:1192
  258.8 44.8 %collective-permute-start.14 = (bf16[512,1536]{1,0:T(8,128)(2,1)}, bf16[512,1536]{1,0:T(8,128)(2,1)}, u32[]{:S(2)}, u32[]{:S(2)}) collective-permute-start(bf16[512,1536]{1,0:T(8,128)(2,1)} %line_land.26.rest_1_.total_home), channel_id=1, source_target_pairs={{1,0},{2,3},{5,4},{6,7},{9,8},{10,11},{13,12},{14,15},{17,16},{18,... | collective-permute-start | bytes 4718600 | tf_op jit(solution)/shard_map/ppermute | solution.py:1192
  260.1 1.1 copy-start.10
  286.5 56.9 %collective-permute-start.22 = (bf16[512,1536]{1,0:T(8,128)(2,1)}, bf16[512,1536]{1,0:T(8,128)(2,1)}, u32[]{:S(2)}, u32[]{:S(2)}) collective-permute-start(bf16[512,1536]{1,0:T(8,128)(2,1)} %get-tuple-element.217.rest_0_.total_home), channel_id=1, source_target_pairs={{0,1},{3,2},{4,5},{7,6},{8,9},{11,10},{12,13},{15,14},{16,17},{19,... | collective-permute-start | bytes 4718600 | tf_op jit(solution)/shard_map/ppermute | solution.py:1192
  293.3 1.2 copy-start.13
  297.3 77.4 %collective-permute-start.20 = (bf16[512,1536]{1,0:T(8,128)(2,1)}, bf16[512,1536]{1,0:T(8,128)(2,1)}, u32[]{:S(2)}, u32[]{:S(2)}) collective-permute-start(bf16[512,1536]{1,0:T(8,128)(2,1)} %line_land.27.rest_0_.total_home), channel_id=1, source_target_pairs={{1,2},{2,1},{5,6},{6,5},{9,10},{10,9},{13,14},{14,13},{17,18},{18,... | collective-permute-start | bytes 4718600 | tf_op jit(solution)/shard_map/ppermute | solution.py:1192
  302.3 76.5 %collective-permute-start.19 = (bf16[512,1536]{1,0:T(8,128)(2,1)}, bf16[512,1536]{1,0:T(8,128)(2,1)S(1)}, u32[]{:S(2)}, u32[]{:S(2)}) collective-permute-start(bf16[512,1536]{1,0:T(8,128)(2,1)} %line_land.28.rest_1_.total_home), channel_id=1, source_target_pairs={{1,0},{2,3},{5,4},{6,7},{9,8},{10,11},{13,12},{14,15},{17,16},{18,... | collective-permute-start | bytes 4718600 | tf_op jit(solution)/shard_map/ppermute | solution.py:1192
  343.4 4.7 copy-start.7
  343.4 12.0 %copy-start.15 = (bf16[256,1536]{1,0:T(8,128)(2,1)S(1)}, bf16[256,1536]{1,0:T(8,128)(2,1)}, u32[]{:S(2)}) copy-start(bf16[256,1536]{1,0:T(8,128)(2,1)} %get-tuple-element.226.total_home) | copy-start | bytes 2359300
  346.2 81.6 %all-reduce.5.cloned.1.call-start = ((), (), s32[]{:S(2)}) async-start(), calls=%async_computation | async-start | bytes 6488064 | tf_op jit(solution)/shard_map/psum | solution.py:1425
  346.3 40.5 %collective-permute-start.24 = (bf16[512,1536]{1,0:T(8,128)(2,1)}, bf16[512,1536]{1,0:T(8,128)(2,1)}, u32[]{:S(2)}, u32[]{:S(2)}) collective-permute-start(bf16[512,1536]{1,0:T(8,128)(2,1)} %line_land.29.rest_0_.total_home), channel_id=1, source_target_pairs={{1,2},{2,1},{5,6},{6,5},{9,10},{10,9},{13,14},{14,13},{17,18},{18,... | collective-permute-start | bytes 4718600 | tf_op jit(solution)/shard_map/ppermute | solution.py:1192
  348.1 24.4 %collective-permute-start.21 = (bf16[256,1536]{1,0:T(8,128)(2,1)S(1)}, bf16[256,1536]{1,0:T(8,128)(2,1)}, u32[]{:S(2)}, u32[]{:S(2)}) collective-permute-start(bf16[256,1536]{1,0:T(8,128)(2,1)S(1)} %copy-done.7), channel_id=1, source_target_pairs={{0,1},{3,2},{4,5},{7,6},{8,9},{11,10},{12,13},{15,14},{16,17},{19,... | collective-permute-start | bytes 2359304 | tf_op jit(solution)/shard_map/ppermute | solution.py:1192
  355.4 29.1 %collective-permute-start.18 = (bf16[256,1536]{1,0:T(8,128)(2,1)S(1)}, bf16[256,1536]{1,0:T(8,128)(2,1)}, u32[]{:S(2)}, u32[]{:S(2)}) collective-permute-start(bf16[256,1536]{1,0:T(8,128)(2,1)S(1)} %copy-done.15), channel_id=1, source_target_pairs={{0,1},{3,2},{4,5},{7,6},{8,9},{11,10},{12,13},{15,14},{16,17},{19,... | collective-permute-start | bytes 2359304 | tf_op jit(solution)/shard_map/ppermute | solution.py:1192
  377.5 39.5 %collective-permute-start.26 = (bf16[512,1536]{1,0:T(8,128)(2,1)}, bf16[512,1536]{1,0:T(8,128)(2,1)}, u32[]{:S(2)}, u32[]{:S(2)}) collective-permute-start(bf16[512,1536]{1,0:T(8,128)(2,1)} %line_land.31.rest_0_.total_home), channel_id=1, source_target_pairs={{1,0},{2,3},{5,4},{6,7},{9,8},{10,11},{13,12},{14,15},{17,16},{18,... | collective-permute-start | bytes 4718600 | tf_op jit(solution)/shard_map/ppermute | solution.py:1192
  378.8 1.1 copy-start.9
  386.7 4.2 copy-start.6
  386.7 5.0 copy-start.5
  389.7 56.4 %collective-permute-start.25 = (bf16[512,1536]{1,0:T(8,128)(2,1)}, bf16[512,1536]{1,0:T(8,128)(2,1)}, u32[]{:S(2)}, u32[]{:S(2)}) collective-permute-start(bf16[512,1536]{1,0:T(8,128)(2,1)} %line_land.33.rest_1_.total_home), channel_id=1, source_target_pairs={{1,0},{2,3},{5,4},{6,7},{9,8},{10,11},{13,12},{14,15},{17,16},{18,... | collective-permute-start | bytes 4718600 | tf_op jit(solution)/shard_map/ppermute | solution.py:1192
  391.0 29.6 %collective-permute-start.27 = (bf16[256,1536]{1,0:T(8,128)(2,1)S(1)}, bf16[256,1536]{1,0:T(8,128)(2,1)S(1)}, u32[]{:S(2)}, u32[]{:S(2)}) collective-permute-start(bf16[256,1536]{1,0:T(8,128)(2,1)S(1)} %copy-done.6), channel_id=1, source_target_pairs={{1,2},{2,1},{5,6},{6,5},{9,10},{10,9},{13,14},{14,13},{17,18},{18,... | collective-permute-start | bytes 2359304 | tf_op jit(solution)/shard_map/ppermute | solution.py:1192
  391.7 57.9 %collective-permute-start.23 = (bf16[256,1536]{1,0:T(8,128)(2,1)S(1)}, bf16[256,1536]{1,0:T(8,128)(2,1)}, u32[]{:S(2)}, u32[]{:S(2)}) collective-permute-start(bf16[256,1536]{1,0:T(8,128)(2,1)S(1)} %copy-done.5), channel_id=1, source_target_pairs={{1,2},{2,1},{5,6},{6,5},{9,10},{10,9},{13,14},{14,13},{17,18},{18,... | collective-permute-start | bytes 2359304 | tf_op jit(solution)/shard_map/ppermute | solution.py:1192
  420.6 7.2 %copy-start.16 = (bf16[256,1536]{1,0:T(8,128)(2,1)}, bf16[256,1536]{1,0:T(8,128)(2,1)S(1)}, u32[]{:S(2)}) copy-start(bf16[256,1536]{1,0:T(8,128)(2,1)S(1)} %collective-permute-done.27.moved_home) | copy-start | bytes 2359300
  427.8 3.6 copy-start.4
  430.1 35.2 %collective-permute-start.29 = (bf16[256,1536]{1,0:T(8,128)(2,1)}, bf16[256,1536]{1,0:T(8,128)(2,1)}, u32[]{:S(2)}, u32[]{:S(2)}) collective-permute-start(bf16[256,1536]{1,0:T(8,128)(2,1)} %line_land.34.rest_1_.total_home), channel_id=1, source_target_pairs={{1,0},{2,3},{5,4},{6,7},{9,8},{10,11},{13,12},{14,15},{17,16},{18,... | collective-permute-start | bytes 2359304 | tf_op jit(solution)/shard_map/ppermute | solution.py:1192
  431.4 2.6 copy-start.3
  434.0 2.8 copy-start.17
  451.8 45.0 %collective-permute-start.28 = (bf16[256,1536]{1,0:T(8,128)(2,1)}, bf16[256,1536]{1,0:T(8,128)(2,1)S(1)}, u32[]{:S(2)}, u32[]{:S(2)}) collective-permute-start(bf16[256,1536]{1,0:T(8,128)(2,1)} %line_land.35.rest_1_.total_home), channel_id=1, source_target_pairs={{1,0},{2,3},{5,4},{6,7},{9,8},{10,11},{13,12},{14,15},{17,16},{18,... | collective-permute-start | bytes 2359304 | tf_op jit(solution)/shard_map/ppermute | solution.py:1192
  468.3 7.3 %copy-start.2 = (bf16[1536,768]{1,0:T(8,128)(2,1)S(1)}, bf16[1536,768]{1,0:T(8,128)(2,1)}, u32[]{:S(2)}) copy-start(bf16[1536,768]{1,0:T(8,128)(2,1)} %get-tuple-element.247.rest_1_) | copy-start | bytes 7077892
  470.6 19.2 %collective-permute-start.30 = (bf16[480,256]{1,0:T(8,128)(2,1)}, bf16[480,256]{1,0:T(8,128)(2,1)S(1)}, u32[]{:S(2)}, u32[]{:S(2)}) collective-permute-start(bf16[480,256]{1,0:T(8,128)(2,1)} %get-tuple-element.239), channel_id=1, source_target_pairs={{0,1},{1,0},{2,3},{3,2},{4,5},{5,4},{6,7},{7,6},{8,9},{9,8},{10,11... | collective-permute-start | bytes 737288 | tf_op jit(solution)/shard_map/ppermute | solution.py:1277
  470.6 19.2 %collective-permute-start.31 = (bf16[480,256]{1,0:T(8,128)(2,1)}, bf16[480,256]{1,0:T(8,128)(2,1)S(1)}, u32[]{:S(2)}, u32[]{:S(2)}) collective-permute-start(bf16[480,256]{1,0:T(8,128)(2,1)} %get-tuple-element.240), channel_id=1, source_target_pairs={{0,2},{1,3},{2,0},{3,1},{4,6},{5,7},{6,4},{7,5},{8,10},{9,11},{10,... | collective-permute-start | bytes 737288 | tf_op jit(solution)/shard_map/ppermute | solution.py:1277
  470.6 19.2 %collective-permute-start.32 = (bf16[480,256]{1,0:T(8,128)(2,1)}, bf16[480,256]{1,0:T(8,128)(2,1)}, u32[]{:S(2)}, u32[]{:S(2)}) collective-permute-start(bf16[480,256]{1,0:T(8,128)(2,1)} %get-tuple-element.241), channel_id=1, source_target_pairs={{0,3},{1,2},{2,1},{3,0},{4,7},{5,6},{6,5},{7,4},{8,11},{9,10},{10,... | collective-permute-start | bytes 737288 | tf_op jit(solution)/shard_map/ppermute | solution.py:1277
  489.8 0.7 copy-start.18
  489.8 0.8 copy-start.19
  496.8 0.9 copy-start.14
Sparse Core Ops, SparseCore 0:
  177.5 87.1 all-reduce.6
  357.7 70.0 all-reduce.4

commit v2 on v1

--- a/solution.py
+++ b/solution.py
@@ -94,6 +94,21 @@
 HBM = pl.BlockSpec(memory_space=pl.ANY)
 SMEM = pl.BlockSpec(memory_space=pltpu.SMEM)
 ANY = pl.BlockSpec(memory_space=pl.ANY)
+
+
+def spread_heads(step_size, levels, begins, ends, owners):
+    end_level = levels[CHUNK - 1 : CHUNK, :]
+    last = jnp.broadcast_to(jnp.exp2(end_level), (8, LANES))
+    compact = jnp.concatenate(
+        [
+            halves(step_size),
+            halves(begins * jnp.exp2(levels)),
+            halves(ends * jnp.exp2(end_level - levels)),
+            halves(last),
+        ],
+        axis=0,
+    )
+    return dot(compact, owners[...])
 
 
 def whole(shape):
@@ -145,6 +160,7 @@
     state_chan,
     heads,
     small_weight,
+    owners,
 ):
     length = segments.shape[0]
     inner = gate_gain.shape[0]
@@ -173,6 +189,8 @@
     channel = lax.broadcasted_iota(jnp.int32, (LANES, inner), 1)
     owns = (channel // (inner // count) == owner).astype(f32)
     chan[5:6, :] = dot(heads[...], owns, highest)[3:4]
+    owners[:LANES, :] = owns.astype(bf16)
+    owners[LANES:, :] = owns.astype(bf16)
     chan[6:7, :] = line_of(gate_gain)
     state_chan[...] = jnp.zeros_like(state_chan)
     state_chan[0:4, :] = state_conv[...]
@@ -190,6 +208,7 @@
         ((8, 256), f32),
         ((8, LANES), f32),
         ((width, 384), bf16),
+        ((2 * LANES, inner), bf16),
     ]
     return pl.pallas_call(
         prepare_kernel,
@@ -216,6 +235,7 @@
     chan,
     state_chan,
     heads,
+    owners,
     *rest,
     block,
     first,
@@ -255,6 +275,7 @@
         out_weight,
         damped,
         carried_out,
+        by_head,
         load_sems,
         store_sems,
     ) = rest
@@ -354,6 +375,7 @@
         state_low = state[...].astype(bf16)
         kept_states[index] = state_low
         carried_out[...] = dot(state_c, state_low)
+        by_head[...] = spread_heads(step_size, levels, begins, ends, owners)
         low = low_lanes()
         squares = jnp.zeros((CHUNK, LANES), f32)
         crosses = jnp.zeros((CHUNK, LANES), f32)
@@ -366,28 +388,23 @@
             mixer_in[at, lanes] = value
             slope[at, lanes] = (sigma + act * (1.0 - sigma)).astype(bf16)
             value = value.astype(f32)
-            level_pair = []
             weights = []
             for h in (2 * j, 2 * j + 1):
                 level = spread(levels[:, h : h + 1])
-                level_pair.append(level)
                 damping = jnp.exp2(jnp.minimum(level - levels_row[h : h + 1, :], 0.0))
                 weights.append((scores * damping).astype(bf16))
-            level = jnp.where(low, level_pair[0], level_pair[1])
-            step_pair = jnp.where(
-                low,
-                spread(step_size[:, 2 * j : 2 * j + 1]),
-                spread(step_size[:, 2 * j + 1 : 2 * j + 2]),
-            )
+            step_pair = by_head[0:CHUNK, lanes]
+            beginning = by_head[CHUNK : 2 * CHUNK, lanes]
+            ending = by_head[2 * CHUNK : 3 * CHUNK, lanes]
+            last = by_head[3 * CHUNK : 3 * CHUNK + 1, lanes]
             stepped = value * step_pair
             stacked = jnp.concatenate(
                 [jnp.where(low, stepped, 0.0), jnp.where(low, 0.0, stepped)], axis=0
             ).astype(bf16)
-            end_level = level[CHUNK - 1 : CHUNK, :]
             result = dot(jnp.concatenate(weights, axis=1), stacked)
-            result += (begins * jnp.exp2(level)) * carried_out[:, lanes]
-            damped[:, lanes] = (stepped * (ends * jnp.exp2(end_level - level))).astype(bf16)
-            state[:, lanes] = state[:, lanes] * (carried * jnp.exp2(end_level))
+            result += beginning * carried_out[:, lanes]
+            damped[:, lanes] = (stepped * ending).astype(bf16)
+            state[:, lanes] = state[:, lanes] * (carried * last)
             result += chan[5:6, lanes] * value
             mixed[at, lanes] = result
             gate = gate_raw[at, lanes].astype(f32)
@@ -429,8 +446,8 @@
 
 
 def forward(block, starts, marks, tokens, grads, params, carry, earlier, after, project):
-    gain, gate_weight, input_weight, small_weight, chan, state_chan, heads, out_weight = params
-    tables = [gain, chan, state_chan, heads]
+    gain, gate_weight, input_weight, small_weight, *tables, out_weight = params
+    tables = [gain, *tables]
     weights = [input_weight, gate_weight, small_weight, out_weight]
     length, width = tokens.shape
     inner = gate_weight.shape[1]
@@ -490,6 +507,7 @@
             *[pltpu.VMEM(item.shape, bf16) for item in weights],
             pltpu.VMEM((CHUNK, inner), bf16),
             pltpu.VMEM((CHUNK, inner), f32),
+            pltpu.VMEM((3 * CHUNK + 8, inner), f32),
             pltpu.SemaphoreType.DMA((6,)),
             pltpu.SemaphoreType.DMA((11,)),
         ],
@@ -598,6 +616,7 @@
     chan,
     state_chan,
     heads,
+    owners,
     *rest,
     block,
     first,
@@ -639,6 +658,7 @@
         normed_grad,
         picks,
         carried_back,
+        by_head,
         load_sems,
         store_sems,
     ) = rest
@@ -718,6 +738,7 @@
         levels_row = jnp.transpose(levels)
         state_low = state_grad[...].astype(bf16)
         carried_back[...] = dot(state_b, state_low)
+        by_head[...] = spread_heads(step_size, levels, begins, ends, owners)
         low = low_lanes()
         score_grad = jnp.zeros((CHUNK, CHUNK), f32)
         level_grad = jnp.zeros((CHUNK, LANES), f32)
@@ -732,30 +753,23 @@
             value = mixer_in[at, lanes].astype(f32)
             skip = chan[5:6, lanes]
             chan_sums[0:8, lanes] += fold(grad * value)
-            step_pair = jnp.where(
-                low,
-                spread(step_size[:, 2 * j : 2 * j + 1]),
-                spread(step_size[:, 2 * j + 1 : 2 * j + 2]),
-            )
+            step_pair = by_head[0:CHUNK, lanes]
+            beginning = by_head[CHUNK : 2 * CHUNK, lanes]
+            ending = by_head[2 * CHUNK : 3 * CHUNK, lanes]
+            last = by_head[3 * CHUNK : 3 * CHUNK + 1, lanes]
             stepped = value * step_pair
             stepped_low = stepped.astype(bf16)
             stacked = jnp.concatenate(
                 [jnp.where(low, grad, 0.0), jnp.where(low, 0.0, grad)], axis=0
             ).astype(bf16)
             cells = dot_nt(stepped_low, stacked)
-            level_pair = []
             weights = []
             for k in range(2):
                 h = 2 * j + k
                 level = spread(levels[:, h : h + 1])
-                level_pair.append(level)
                 damping = jnp.exp2(jnp.minimum(levels_row[h : h + 1, :] - level, 0.0))
                 weights.append((scores * damping).astype(bf16))
                 score_grad += cells[:, k * CHUNK : (k + 1) * CHUNK] * damping
-            level = jnp.where(low, level_pair[0], level_pair[1])
-            end_level = level[CHUNK - 1 : CHUNK, :]
-            ending = ends * jnp.exp2(end_level - level)
-            beginning = begins * jnp.exp2(level)
             within = dot(jnp.concatenate(weights, axis=1), stacked)
             beyond = ending * carried_back[:, lanes]
             value_grad = within + beyond
@@ -764,7 +778,7 @@
             behind = state_grad[:, lanes]
             crossing = fold(behind * kept_states[index, :, lanes].astype(f32))
             crossing_sum += dot(halves(crossing), pick)
-            state_grad[:, lanes] = behind * (carried * jnp.exp2(end_level))
+            state_grad[:, lanes] = behind * (carried * last)
             rows_flow = grad * (mix - skip * value) - stepped_low.astype(f32) * within
             level_grad += dot(halves(rows_flow), pick)
             inter_grad += dot((stepped * beyond).astype(bf16), pick[:LANES])
@@ -871,8 +885,8 @@
 
 
 def backward(block, starts, marks, tokens, params, saved, grads, carry, earlier, after, parts):
-    gain, gate_weight, input_weight, small_weight, chan, state_chan, heads, _ = params
-    tables = [gain, chan, state_chan, heads]
+    gain, gate_weight, input_weight, small_weight, *tables, _ = params
+    tables = [gain, *tables]
     length, width = tokens.shape
     inner = gate_weight.shape[1]
     chunks = ROWS // CHUNK
@@ -949,6 +963,7 @@
             pltpu.VMEM((ROWS, width), f32),
             pltpu.VMEM((inner // LANES, 2 * LANES, LANES), bf16),
             pltpu.VMEM((CHUNK, inner), f32),
+            pltpu.VMEM((3 * CHUNK + 8, inner), f32),
             pltpu.SemaphoreType.DMA((22,)),
             pltpu.SemaphoreType.DMA((2,)),
         ],
@@ -1318,7 +1333,7 @@
     columns = width // groups
     total_inner = inner * groups
 
-    gain, marks, chan, state_chan, heads, small_weight = prepare(
+    gain, marks, chan, state_chan, heads, small_weight, owners = prepare(
         length,
         width,
         inner,
@@ -1345,6 +1360,7 @@
         chan,
         state_chan,
         heads,
+        owners,
         out_weight,
     )
     blocks = length // ROWS
@@ -1413,6 +1429,8 @@
             line.push(partial, "input", block * ROWS + k * partial.shape[0])
         if block > 0:
             after = line.tick(ending, after)
+        else:
+            after = line.tick(ending, after, then=0, last=0)
     mixer_low, small_low = lows
     chan_sums, state_sums, head_sums, gain_sums = carry[2:]
     weight_sums = weight_grads(
@@ -1423,7 +1441,7 @@
     )
     after = [weight_sums[0]]
     input_weight_grad, state_weight_grad, packed = lax.psum(tuple(weight_sums), "dp")
-    after = line.tick(ending, after, first=2)
+    after = line.tick(ending, after, first=2, then=2)
     ticks = 0
     while line.busy():
         after = after + [input_weight_grad] if ticks == 1 else after

time: 515 us -> 512 us (level)
  starting transfers between devices: 81.6 us -> 75.7 us
    psum x1, waiting for transfers between devices: 7.14 us -> 21.2 us  [on_device(): lax.psum(tuple(weight_sums), 'dp')]
    ppermute x3, waiting for transfers between devices: 9.1 us -> 0.01 us  [sum_pieces(): lax.ppermute(sent[k - 1], axis, [(i, i ^ k) for i in range(size)])]
    ppermute x27, starting transfers between devices: 72.8 us -> 66.7 us  [launch(): moved = lax.ppermute(total, 'tensor', self.steps[step][1])]
    ppermute x27, waiting for transfers between devices: 61.7 us -> 55.7 us  [launch(): moved = lax.ppermute(total, 'tensor', self.steps[step][1])]
    unnamed x52 -> x56, local copies, waits for them, and re-layouts: 10.7 us -> 13.6 us
  transfers between devices with their start and end apart: 35 -> 35, of which waited for: 9 -> 8; matrix products, arithmetic and copies ran while one was open for 4% -> 3% of each run, Pallas kernels for 52% -> 53%
where the time goes in v2:
time: 512 us; the launch traced here: 505 us
  Pallas kernels  298 us (58%)
  waiting for transfers between devices  85.6 us (17%)
  starting transfers between devices  75.7 us (15%)
  local copies, waits for them, and re-layouts  21.5 us (4%)
  between operations  15 us (3%)
  other arithmetic  9.9 us (2%)
    pallas_call x4, Pallas kernels, backward(): pl.pallas_call(functools.partial(backward_kernel, block=block, first=not...  87.8 us
    pallas_call x4, Pallas kernels, forward(): pl.pallas_call(functools.partial(forward_kernel, block=block, first=not c...  72.2 us
    ppermute x27, starting transfers between devices, launch(): moved = lax.ppermute(total, 'tensor', self.steps[step][1])  66.7 us
    ppermute x27, waiting for transfers between devices, launch(): moved = lax.ppermute(total, 'tensor', self.steps[step][1])  55.7 us
    pallas_call x18, Pallas kernels, land(): pl.pallas_call(functools.partial(land_kernel, mode=mode, unread=len(after...  47.9 us
    pallas_call x3, Pallas kernels, weight_grads(): pl.pallas_call(functools.partial(weight_kernel, rights=len(rights), unrea...  33.6 us
    pallas_call x9, Pallas kernels, finish(): pl.pallas_call(functools.partial(finish_kernel, adds=adds, inner=inner, r...  31.3 us
    psum x1, waiting for transfers between devices, on_device(): lax.psum(tuple(weight_sums), 'dp')  21.2 us
  transfers between devices with their start and end apart: 35, of which 8 were waited for; matrix products, arithmetic and copies ran while one was open for 3% of the time, Pallas kernels for 53%

profile of v2, /device:TPU:0, one launch (start us, length us, event | category | flops | bytes accessed | tf_op | source)
XLA Modules:
  0.0 505.3 jit_solution(15581259096645006976)
XLA Ops:
  8.9 2.9 prepare.1
  11.8 18.0 %forward_mix.4 = (bf16[2048,1536]{1,0:T(8,128)(2,1)}, bf16[2048,768]{1,0:T(8,128)(2,1)}, bf16[2048,768]{1,0:T(8,128)(2,1)}, bf16[2048,384]{1,0:T(8,128)(2,1)}, b...) custom-call(s32[2048]{0:T(1024)} %starts.15, ...), custom_call_target="tpu_custom_call" | custom-call | flops 1000 | bytes 1000 | tf_op jit(solution)/shard_map/forward_mix/pallas_call | solution.py:486
  29.8 5.3 %collective-permute-start = (bf16[512,1536]{1,0:T(8,128)(2,1)}, bf16[512,1536]{1,0:T(8,128)(2,1)S(1)}, u32[]{:S(2)}, u32[]{:S(2)}) collective-permute-start(bf16[512,1536]{1,0:T(8,128)(2,1)} %get-tuple-element.151.rest_13_.total_home), channel_id=1, source_target_pairs={{0,1},{3,2},{4,5},{7,6},{8,9},{11,10},{12,13},{15,14},{16,17},{19,... | collective-permute-start | bytes 4718600 | tf_op jit(solution)/shard_map/ppermute | solution.py:1207
  35.1 18.2 %forward_mix.5 = (bf16[2048,1536]{1,0:T(8,128)(2,1)}, bf16[2048,768]{1,0:T(8,128)(2,1)}, bf16[2048,768]{1,0:T(8,128)(2,1)}, bf16[2048,384]{1,0:T(8,128)(2,1)}, b...) custom-call(s32[2048]{0:T(1024)} %starts.15, ...), custom_call_target="tpu_custom_call", output_to_operand_aliasing={{0}: (15, {}), {1}: (16, {}), {2}: (17, {}), {3}: (18, {}),... | custom-call | flops 1000 | bytes 1000 | tf_op jit(solution)/shard_map/forward_mix/pallas_call | solution.py:486
  54.8 17.9 %forward_mix.6 = (bf16[2048,1536]{1,0:T(8,128)(2,1)}, bf16[2048,768]{1,0:T(8,128)(2,1)}, bf16[2048,768]{1,0:T(8,128)(2,1)}, bf16[2048,384]{1,0:T(8,128)(2,1)}, b...) custom-call(s32[2048]{0:T(1024)} %starts.15, ...), custom_call_target="tpu_custom_call", output_to_operand_aliasing={{0}: (15, {}), {1}: (16, {}), {2}: (17, {}), {3}: (18, {}),... | custom-call | flops 1000 | bytes 1000 | tf_op jit(solution)/shard_map/forward_mix/pallas_call | solution.py:486
  74.0 2.7 line_land.18.rest_13_.total_home
  78.1 18.0 %forward_mix.7 = (bf16[2048,1536]{1,0:T(8,128)(2,1)}, bf16[2048,768]{1,0:T(8,128)(2,1)}, bf16[2048,768]{1,0:T(8,128)(2,1)}, bf16[2048,384]{1,0:T(8,128)(2,1)}, b...) custom-call(s32[2048]{0:T(1024)} %starts.15, ...), custom_call_target="tpu_custom_call", output_to_operand_aliasing={{0}: (15, {}), {1}: (16, {}), {2}: (17, {}), {3}: (18, {}),... | custom-call | flops 1000 | bytes 1000 | tf_op jit(solution)/shard_map/forward_mix/pallas_call | solution.py:486
  98.9 2.5 collective-permute-start.5
  104.1 2.7 line_land.19.rest_0_.total_home
  106.8 7.9 %collective-permute-done.4 = f32[2,2048]{1,0:T(2,128)S(1)} collective-permute-done((f32[2,2048]{1,0:T(2,128)S(1)}, f32[2,2048]{1,0:T(2,128)S(1)}, u32[]{:S(2)}, u32[]{:S(2)}) %collective-permute-start.4) | collective-permute-done | bytes 16416 | tf_op jit(solution)/shard_map/ppermute | solution.py:1250
  117.4 2.7 line_land.20.refs_3_.total_home
  120.1 5.7 %project_rows.1 = (bf16[512,1536]{1,0:T(8,128)(2,1)}, bf16[512,1536]{1,0:T(8,128)(2,1)}) custom-call(bf16[512,768]{1,0:T(8,128)(2,1)} %get-tuple-element.166.rest_0_.refs_0_, bf16[512,768]{1,0:T(8,128)(2,1)} %get-tuple-element.180.refs_1_, bf16[768,1536]{1,0:T(8,128)(2,1)} %refs_2_.1, bf16[512,1536]{1,0:T(8,128)(2,1)} %line_land.20.refs_3_.total_home, ...), custom_call_target="tpu_custom_call" | custom-call | flops 1000 | bytes 1000 | tf_op jit(solution)/shard_map/project_rows/pallas_call | solution.py:534
  125.8 3.8 collective-permute-start.9
  132.7 6.8 %collective-permute-start.6 = (bf16[512,1536]{1,0:T(8,128)(2,1)}, bf16[512,1536]{1,0:T(8,128)(2,1)}, u32[]{:S(2)}, u32[]{:S(2)}) collective-permute-start(bf16[512,1536]{1,0:T(8,128)(2,1)} %get-tuple-element.185.total_home), channel_id=1, source_target_pairs={{0,1},{3,2},{4,5},{7,6},{8,9},{11,10},{12,13},{15,14},{16,17},{19,... | collective-permute-start | bytes 4718600 | tf_op jit(solution)/shard_map/ppermute | solution.py:1207
  139.6 11.6 %gate_grads.1 = (bf16[2048,768]{1,0:T(8,128)(2,1)}, bf16[2048,768]{1,0:T(8,128)(2,1)}, bf16[2048,768]{1,0:T(8,128)(2,1)}, f32[8,768]{1,0:T(8,128)}) custom-call(f32[2,2048]{1,0:T(2,128)} %add_add_fusion.refs_4_.sums, f32[2048,768]{1,0:T(8,128)} %get-tuple-element.186.mixed.rest_0_, bf16[2048,768]{1,0:T(8,128)(2,1)} %get-tuple-element.187.gate_raw, ...), custom_call_target="tpu_custom_call" | custom-call | flops 1000 | bytes 1000 | tf_op jit(solution)/shard_map/gate_grads/pallas_call | solution.py:592
  151.2 9.5 %weight_grads.3.rest_1_ = bf16[1536,768]{1,0:T(8,128)(2,1)} custom-call(bf16[2048,1536]{1,0:T(8,128)(2,1)} %get-tuple-element.200.left, bf16[2048,768]{1,0:T(8,128)(2,1)} %get-tuple-element.198.rest_0_.rest_9_, bf16[2048,768]{1,0:T(8,128)(2,1)} %get-tuple-element.190.rest_1_), custom_call_target="tpu_custom_call" | custom-call | flops 1000 | bytes 1000 | tf_op jit(solution)/shard_map/weight_grads/pallas_call | solution.py:1030
  160.7 9.5 %weight_grads.4.rest_0_ = bf16[768,1536]{1,0:T(8,128)(2,1)} custom-call(bf16[2048,768]{1,0:T(8,128)(2,1)} %get-tuple-element.199.left, bf16[2048,1536]{1,0:T(8,128)(2,1)} %base_home.17, bf16[1536,768]{1,0:T(8,128)(2,1)} %weight_grads.3.rest_1_), custom_call_target="tpu_custom_call" | custom-call | flops 1000 | bytes 1000 | tf_op jit(solution)/shard_map/weight_grads/pallas_call | solution.py:1030
  170.3 2.8 line_land.21.rest_0_.total_home
  174.9 2.7 line_land.22.rest_0_.total_home
  179.0 3.7 line_finish.9.rest_14_.rest_0_
  182.7 21.8 %backward_mix.4 = (bf16[2048,768]{1,0:T(8,128)(2,1)}, bf16[2048,384]{1,0:T(8,128)(2,1)}, bf16[512,1536]{1,0:T(8,128)(2,1)}, f32[128,768]{1,0:T(8,128)}, f32[8,10...) custom-call(s32[2048]{0:T(1024)} %starts.15, ...), custom_call_target="tpu_custom_call" | custom-call | flops 1000 | bytes 1000 | tf_op jit(solution)/shard_map/backward_mix/pallas_call | solution.py:928
  204.5 5.8 %collective-permute-start.11 = (bf16[512,1536]{1,0:T(8,128)(2,1)}, bf16[512,1536]{1,0:T(8,128)(2,1)}, u32[]{:S(2)}, u32[]{:S(2)}) collective-permute-start(bf16[512,1536]{1,0:T(8,128)(2,1)} %get-tuple-element.201.rest_0_.total_home), channel_id=1, source_target_pairs={{0,1},{3,2},{4,5},{7,6},{8,9},{11,10},{12,13},{15,14},{16,17},{19,... | collective-permute-start | bytes 4718600 | tf_op jit(solution)/shard_map/ppermute | solution.py:1207
  210.3 2.8 line_land.23.rest_0_.total_home
  214.9 2.8 line_land.24.rest_1_.total_home
  220.1 3.7 line_finish.10.rest_22_.rest_0_
  223.9 22.1 %backward_mix.5 = (bf16[2048,768]{1,0:T(8,128)(2,1)}, bf16[2048,384]{1,0:T(8,128)(2,1)}, bf16[512,1536]{1,0:T(8,128)(2,1)}, f32[128,768]{1,0:T(8,128)}, f32[8,10...) custom-call(s32[2048]{0:T(1024)} %starts.15, ...), custom_call_target="tpu_custom_call", output_to_operand_aliasing={{0}: (27, {}), {1}: (28, {})} | custom-call | flops 1000 | bytes 1000 | tf_op jit(solution)/shard_map/backward_mix/pallas_call | solution.py:928
  245.9 5.9 %collective-permute-start.17 = (bf16[512,1536]{1,0:T(8,128)(2,1)}, bf16[512,1536]{1,0:T(8,128)(2,1)}, u32[]{:S(2)}, u32[]{:S(2)}) collective-permute-start(bf16[512,1536]{1,0:T(8,128)(2,1)} %get-tuple-element.210.rest_0_.total_home), channel_id=1, source_target_pairs={{0,1},{3,2},{4,5},{7,6},{8,9},{11,10},{12,13},{15,14},{16,17},{19,... | collective-permute-start | bytes 4718600 | tf_op jit(solution)/shard_map/ppermute | solution.py:1207
  251.8 2.8 line_land.25.rest_0_.total_home
  256.5 2.8 line_land.26.rest_1_.total_home
  261.8 3.6 line_finish.11.rest_22_.rest_0_
  265.4 22.0 %backward_mix.6 = (bf16[2048,768]{1,0:T(8,128)(2,1)}, bf16[2048,384]{1,0:T(8,128)(2,1)}, bf16[512,1536]{1,0:T(8,128)(2,1)}, f32[128,768]{1,0:T(8,128)}, f32[8,10...) custom-call(s32[2048]{0:T(1024)} %starts.15, ...), custom_call_target="tpu_custom_call", output_to_operand_aliasing={{0}: (27, {}), {1}: (28, {})} | custom-call | flops 1000 | bytes 1000 | tf_op jit(solution)/shard_map/backward_mix/pallas_call | solution.py:928
  287.4 4.7 collective-permute-start.20
  292.1 2.8 line_land.27.rest_0_.total_home
  294.9 2.2 collective-permute-start.22
  297.1 2.8 line_land.28.rest_1_.total_home
  301.0 3.6 line_finish.12.rest_22_
  304.6 21.9 %backward_mix.7 = (bf16[2048,768]{1,0:T(8,128)(2,1)}, bf16[2048,384]{1,0:T(8,128)(2,1)}, bf16[256,1536]{1,0:T(8,128)(2,1)}, bf16[256,1536]{1,0:T(8,128)(2,1)}, f...) custom-call(s32[2048]{0:T(1024)} %starts.15, ...), custom_call_target="tpu_custom_call", output_to_operand_aliasing={{0}: (27, {}), {1}: (28, {})} | custom-call | flops 1000 | bytes 1000 | tf_op jit(solution)/shard_map/backward_mix/pallas_call | solution.py:928
  327.7 2.9 line_land.29.rest_7_.total_home
  332.5 3.4 collective-permute-start.19
  335.9 2.2 collective-permute-start.18
  339.4 14.6 %weight_grads.5 = (bf16[1536,768]{1,0:T(8,128)(2,1)}, bf16[1536,256]{1,0:T(8,128)(2,1)}, bf16[32,1536]{1,0:T(8,128)(2,1)}) custom-call(bf16[2048,1536]{1,0:T(8,128)(2,1)} %get-tuple-element.200.left, bf16[2048,768]{1,0:T(8,128)(2,1)} %get-tuple-element.230.rest_0_, bf16[2048,384]{1,0:T(8,128)(2,1)} %get-tuple-element.231.rest_1_, ...), custom_call_target="tpu_custom_call" | custom-call | flops 1000 | bytes 1000 | tf_op jit(solution)/shard_map/weight_grads/pallas_call | solution.py:1030
  354.9 2.2 line_land.30.rest_0_.total_home
  357.8 8.8 %collective-permute-done.18.moved_home = bf16[256,1536]{1,0:T(8,128)(2,1)} collective-permute-done((bf16[256,1536]{1,0:T(8,128)(2,1)}, bf16[256,1536]{1,0:T(8,128)(2,1)}, u32[]{:S(2)}, u32[]{:S(2)}) %collective-permute-start.18) | collective-permute-done | bytes 786464 | tf_op jit(solution)/shard_map/ppermute | solution.py:1207
  366.7 2.2 line_land.31.rest_0_.total_home
  368.9 2.9 line_land.32.rest_0_.total_home
  374.6 2.8 line_land.33.rest_0_.total_home
  380.3 3.7 line_finish.13.rest_0_
  384.1 2.4 line_land.34.rest_1_.total_home
  387.8 2.5 convert_element_type.15
  390.3 2.8 convert_element_type.18
  393.2 18.6 %collective-permute-done.23.moved_home = bf16[512,1536]{1,0:T(8,128)(2,1)} collective-permute-done((bf16[512,1536]{1,0:T(8,128)(2,1)}, bf16[512,1536]{1,0:T(8,128)(2,1)}, u32[]{:S(2)}, u32[]{:S(2)}) %collective-permute-start.23) | collective-permute-done | bytes 1572896 | tf_op jit(solution)/shard_map/ppermute | solution.py:1207
  411.7 3.5 line_finish.14.rest_0_
  415.3 21.2 %all-reduce.5.cloned.1.call-done = (bf16[1536,768]{1,0:T(8,128)(2,1)}, bf16[32,1536]{1,0:T(8,128)(2,1)}, bf16[1536,256]{1,0:T(8,128)(2,1)}) async-done(((bf16[1536,768]{1,0:T(8,128)(2,1)}, bf16[32,1536]{1,0:T(8,128)(2,1)}, bf16[1536,256]{1,0:T(8,128)(2,1)}), (bf16[1536,768]{1,0:T(8,128)(2,1)}, bf16[32,1536]{1,0:T(8,128)(2,1)}, bf16[1536,256]{1,0:T(8,128)(2,1)})) %all-reduce.5.cloned.1.call-update) | async-done | bytes 3244048 | tf_op jit(solution)/shard_map/psum | solution.py:1443
  436.5 2.3 line_land.35.rest_1_.total_home
  440.8 4.7 collective-permute-done.29.moved_home
  445.4 3.5 line_finish.15.rest_0_
  449.0 13.2 %collective-permute-done.28.moved_home = bf16[256,1536]{1,0:T(8,128)(2,1)S(1)} collective-permute-done((bf16[256,1536]{1,0:T(8,128)(2,1)}, bf16[256,1536]{1,0:T(8,128)(2,1)S(1)}, u32[]{:S(2)}, u32[]{:S(2)}) %collective-permute-start.28) | collective-permute-done | bytes 786464 | tf_op jit(solution)/shard_map/ppermute | solution.py:1207
  463.1 3.0 line_finish.16.rest_0_
  466.1 2.3 part_pieces.1
  468.4 3.0 collective-permute-start.31
  473.4 2.5 convert_element_type.16
  478.5 8.7 %collective-permute-done.27.moved_home = bf16[256,1536]{1,0:T(8,128)(2,1)S(1)} collective-permute-done((bf16[256,1536]{1,0:T(8,128)(2,1)}, bf16[256,1536]{1,0:T(8,128)(2,1)S(1)}, u32[]{:S(2)}, u32[]{:S(2)}) %collective-permute-start.27) | collective-permute-done | bytes 786464 | tf_op jit(solution)/shard_map/ppermute | solution.py:1207
  488.1 3.0 line_finish.17
  492.0 2.2 join_pieces.1
  (124 shorter events, 55.9 us)
Async XLA Ops:
  29.8 42.9 %collective-permute-start = (bf16[512,1536]{1,0:T(8,128)(2,1)}, bf16[512,1536]{1,0:T(8,128)(2,1)S(1)}, u32[]{:S(2)}, u32[]{:S(2)}) collective-permute-start(bf16[512,1536]{1,0:T(8,128)(2,1)} %get-tuple-element.151.rest_13_.total_home), channel_id=1, source_target_pairs={{0,1},{3,2},{4,5},{7,6},{8,9},{11,10},{12,13},{15,14},{16,17},{19,... | collective-permute-start | bytes 4718600 | tf_op jit(solution)/shard_map/ppermute | solution.py:1207
  53.4 49.6 %collective-permute-start.2 = (bf16[512,1536]{1,0:T(8,128)(2,1)}, bf16[512,1536]{1,0:T(8,128)(2,1)S(1)}, u32[]{:S(2)}, u32[]{:S(2)}) collective-permute-start(bf16[512,1536]{1,0:T(8,128)(2,1)} %get-tuple-element.165.rest_13_.total_home), channel_id=1, source_target_pairs={{0,1},{3,2},{4,5},{7,6},{8,9},{11,10},{12,13},{15,14},{16,17},{19,... | collective-permute-start | bytes 4718600 | tf_op jit(solution)/shard_map/ppermute | solution.py:1207
  72.7 1.2 copy-start.13
  73.9 4.1 copy-start.23
  73.9 4.1 copy-start.24
  73.9 4.1 copy-start.25
  76.7 39.4 %collective-permute-start.1 = (bf16[512,1536]{1,0:T(8,128)(2,1)}, bf16[512,1536]{1,0:T(8,128)(2,1)S(1)}, u32[]{:S(2)}, u32[]{:S(2)}) collective-permute-start(bf16[512,1536]{1,0:T(8,128)(2,1)} %line_land.18.rest_13_.total_home), channel_id=1, source_target_pairs={{1,2},{2,1},{5,6},{6,5},{9,10},{10,9},{13,14},{14,13},{17,18},{18,... | collective-permute-start | bytes 4718600 | tf_op jit(solution)/shard_map/ppermute | solution.py:1207
  96.8 6.2 %copy-start.22 = (f32[2,2048]{1,0:T(2,128)}, f32[2,2048]{1,0:T(2,128)S(1)}, u32[]{:S(2)}) copy-start(f32[2,2048]{1,0:T(2,128)S(1)} %constant_dynamic-update-slice_fusion.rest_0_) | copy-start | bytes 49156
  96.8 18.0 %collective-permute-start.4 = (f32[2,2048]{1,0:T(2,128)S(1)}, f32[2,2048]{1,0:T(2,128)S(1)}, u32[]{:S(2)}, u32[]{:S(2)}) collective-permute-start(f32[2,2048]{1,0:T(2,128)S(1)} %constant_dynamic-update-slice_fusion.rest_0_), channel_id=1, source_target_pairs={{0,2},{1,3},{2,0},{3,1},{4,6},{5,7},{6,4},{7,5},{8,10},{9,11},{10,... | collective-permute-start | bytes 49160 | tf_op jit(solution)/shard_map/ppermute | solution.py:1250
  98.9 15.9 %collective-permute-start.5 = (f32[2,2048]{1,0:T(2,128)S(1)}, f32[2,2048]{1,0:T(2,128)S(1)}, u32[]{:S(2)}, u32[]{:S(2)}) collective-permute-start(f32[2,2048]{1,0:T(2,128)S(1)} %constant_dynamic-update-slice_fusion.rest_0_), channel_id=1, source_target_pairs={{0,3},{1,2},{2,1},{3,0},{4,7},{5,6},{6,5},{7,4},{8,11},{9,10},{10,... | collective-permute-start | bytes 49160 | tf_op jit(solution)/shard_map/ppermute | solution.py:1250
  101.3 13.4 %collective-permute-start.3 = (f32[2,2048]{1,0:T(2,128)S(1)}, f32[2,2048]{1,0:T(2,128)S(1)}, u32[]{:S(2)}, u32[]{:S(2)}) collective-permute-start(f32[2,2048]{1,0:T(2,128)S(1)} %constant_dynamic-update-slice_fusion.rest_0_), channel_id=1, source_target_pairs={{0,1},{1,0},{2,3},{3,2},{4,5},{5,4},{6,7},{7,6},{8,9},{9,8},{10,11... | collective-permute-start | bytes 49160 | tf_op jit(solution)/shard_map/ppermute | solution.py:1250
  102.9 1.2 copy-start.8
  116.1 1.2 copy-start.12
  120.1 9.5 %copy-start.1 = (bf16[512,1536]{1,0:T(8,128)(2,1)S(1)}, bf16[512,1536]{1,0:T(8,128)(2,1)}, u32[]{:S(2)}) copy-start(bf16[512,1536]{1,0:T(8,128)(2,1)} %line_land.19.rest_0_.total_home) | copy-start | bytes 4718596
  120.1 11.3 %copy-start.2 = (bf16[512,1536]{1,0:T(8,128)(2,1)S(1)}, bf16[512,1536]{1,0:T(8,128)(2,1)}, u32[]{:S(2)}) copy-start(bf16[512,1536]{1,0:T(8,128)(2,1)} %line_land.20.refs_3_.total_home) | copy-start | bytes 4718596
  125.8 44.4 %collective-permute-start.9 = (bf16[512,1536]{1,0:T(8,128)(2,1)}, bf16[512,1536]{1,0:T(8,128)(2,1)}, u32[]{:S(2)}, u32[]{:S(2)}) collective-permute-start(bf16[512,1536]{1,0:T(8,128)(2,1)} %get-tuple-element.189.rest_0_.total_home), channel_id=1, source_target_pairs={{0,1},{3,2},{4,5},{7,6},{8,9},{11,10},{12,13},{15,14},{16,17},{19,... | collective-permute-start | bytes 4718600 | tf_op jit(solution)/shard_map/ppermute | solution.py:1207
  129.6 45.3 %collective-permute-start.8 = (bf16[512,1536]{1,0:T(8,128)(2,1)S(1)}, bf16[512,1536]{1,0:T(8,128)(2,1)}, u32[]{:S(2)}, u32[]{:S(2)}) collective-permute-start(bf16[512,1536]{1,0:T(8,128)(2,1)S(1)} %copy-done.1), channel_id=1, source_target_pairs={{1,2},{2,1},{5,6},{6,5},{9,10},{10,9},{13,14},{14,13},{17,18},{18,... | collective-permute-start | bytes 4718600 | tf_op jit(solution)/shard_map/ppermute | solution.py:1207
  131.4 47.6 %collective-permute-start.7 = (bf16[512,1536]{1,0:T(8,128)(2,1)S(1)}, bf16[512,1536]{1,0:T(8,128)(2,1)}, u32[]{:S(2)}, u32[]{:S(2)}) collective-permute-start(bf16[512,1536]{1,0:T(8,128)(2,1)S(1)} %copy-done.2), channel_id=1, source_target_pairs={{1,0},{2,3},{5,4},{6,7},{9,8},{10,11},{13,12},{14,15},{17,16},{18,... | collective-permute-start | bytes 4718600 | tf_op jit(solution)/shard_map/ppermute | solution.py:1207
  132.7 77.6 %collective-permute-start.6 = (bf16[512,1536]{1,0:T(8,128)(2,1)}, bf16[512,1536]{1,0:T(8,128)(2,1)}, u32[]{:S(2)}, u32[]{:S(2)}) collective-permute-start(bf16[512,1536]{1,0:T(8,128)(2,1)} %get-tuple-element.185.total_home), channel_id=1, source_target_pairs={{0,1},{3,2},{4,5},{7,6},{8,9},{11,10},{12,13},{15,14},{16,17},{19,... | collective-permute-start | bytes 4718600 | tf_op jit(solution)/shard_map/ppermute | solution.py:1207
  173.0 92.3 %all-reduce.7.cloned.1.call-start = ((), (), s32[]{:S(2)}) async-start(), calls=%async_computation.1 | async-start | bytes 9437184 | tf_op jit(solution)/shard_map/psum | solution.py:1410
  173.1 41.8 %collective-permute-start.13 = (bf16[512,1536]{1,0:T(8,128)(2,1)}, bf16[512,1536]{1,0:T(8,128)(2,1)}, u32[]{:S(2)}, u32[]{:S(2)}) collective-permute-start(bf16[512,1536]{1,0:T(8,128)(2,1)} %line_land.21.rest_0_.total_home), channel_id=1, source_target_pairs={{1,2},{2,1},{5,6},{6,5},{9,10},{10,9},{13,14},{14,13},{17,18},{18,... | collective-permute-start | bytes 4718600 | tf_op jit(solution)/shard_map/ppermute | solution.py:1207
  177.7 41.3 %collective-permute-start.12 = (bf16[512,1536]{1,0:T(8,128)(2,1)}, bf16[512,1536]{1,0:T(8,128)(2,1)S(1)}, u32[]{:S(2)}, u32[]{:S(2)}) collective-permute-start(bf16[512,1536]{1,0:T(8,128)(2,1)} %line_land.22.rest_0_.total_home), channel_id=1, source_target_pairs={{1,0},{2,3},{5,4},{6,7},{9,8},{10,11},{13,12},{14,15},{17,16},{18,... | collective-permute-start | bytes 4718600 | tf_op jit(solution)/shard_map/ppermute | solution.py:1207
  204.5 47.3 %collective-permute-start.11 = (bf16[512,1536]{1,0:T(8,128)(2,1)}, bf16[512,1536]{1,0:T(8,128)(2,1)}, u32[]{:S(2)}, u32[]{:S(2)}) collective-permute-start(bf16[512,1536]{1,0:T(8,128)(2,1)} %get-tuple-element.201.rest_0_.total_home), channel_id=1, source_target_pairs={{0,1},{3,2},{4,5},{7,6},{8,9},{11,10},{12,13},{15,14},{16,17},{19,... | collective-permute-start | bytes 4718600 | tf_op jit(solution)/shard_map/ppermute | solution.py:1207
  213.1 43.4 %collective-permute-start.10 = (bf16[512,1536]{1,0:T(8,128)(2,1)}, bf16[512,1536]{1,0:T(8,128)(2,1)}, u32[]{:S(2)}, u32[]{:S(2)}) collective-permute-start(bf16[512,1536]{1,0:T(8,128)(2,1)} %line_land.23.rest_0_.total_home), channel_id=1, source_target_pairs={{1,2},{2,1},{5,6},{6,5},{9,10},{10,9},{13,14},{14,13},{17,18},{18,... | collective-permute-start | bytes 4718600 | tf_op jit(solution)/shard_map/ppermute | solution.py:1207
  217.7 42.9 %collective-permute-start.15 = (bf16[512,1536]{1,0:T(8,128)(2,1)}, bf16[512,1536]{1,0:T(8,128)(2,1)S(1)}, u32[]{:S(2)}, u32[]{:S(2)}) collective-permute-start(bf16[512,1536]{1,0:T(8,128)(2,1)} %line_land.24.rest_1_.total_home), channel_id=1, source_target_pairs={{1,0},{2,3},{5,4},{6,7},{9,8},{10,11},{13,12},{14,15},{17,16},{18,... | collective-permute-start | bytes 4718600 | tf_op jit(solution)/shard_map/ppermute | solution.py:1207
  219.0 1.1 copy-start.11
  245.9 46.2 %collective-permute-start.17 = (bf16[512,1536]{1,0:T(8,128)(2,1)}, bf16[512,1536]{1,0:T(8,128)(2,1)}, u32[]{:S(2)}, u32[]{:S(2)}) collective-permute-start(bf16[512,1536]{1,0:T(8,128)(2,1)} %get-tuple-element.210.rest_0_.total_home), channel_id=1, source_target_pairs={{0,1},{3,2},{4,5},{7,6},{8,9},{11,10},{12,13},{15,14},{16,17},{19,... | collective-permute-start | bytes 4718600 | tf_op jit(solution)/shard_map/ppermute | solution.py:1207
  254.6 42.4 %collective-permute-start.16 = (bf16[512,1536]{1,0:T(8,128)(2,1)}, bf16[512,1536]{1,0:T(8,128)(2,1)}, u32[]{:S(2)}, u32[]{:S(2)}) collective-permute-start(bf16[512,1536]{1,0:T(8,128)(2,1)} %line_land.25.rest_0_.total_home), channel_id=1, source_target_pairs={{1,2},{2,1},{5,6},{6,5},{9,10},{10,9},{13,14},{14,13},{17,18},{18,... | collective-permute-start | bytes 4718600 | tf_op jit(solution)/shard_map/ppermute | solution.py:1207
  259.3 40.6 %collective-permute-start.14 = (bf16[512,1536]{1,0:T(8,128)(2,1)}, bf16[512,1536]{1,0:T(8,128)(2,1)S(1)}, u32[]{:S(2)}, u32[]{:S(2)}) collective-permute-start(bf16[512,1536]{1,0:T(8,128)(2,1)} %line_land.26.rest_1_.total_home), channel_id=1, source_target_pairs={{1,0},{2,3},{5,4},{6,7},{9,8},{10,11},{13,12},{14,15},{17,16},{18,... | collective-permute-start | bytes 4718600 | tf_op jit(solution)/shard_map/ppermute | solution.py:1207
  260.6 1.2 copy-start.10
  287.4 39.2 %collective-permute-start.20 = (bf16[512,1536]{1,0:T(8,128)(2,1)}, bf16[512,1536]{1,0:T(8,128)(2,1)S(1)}, u32[]{:S(2)}, u32[]{:S(2)}) collective-permute-start(bf16[512,1536]{1,0:T(8,128)(2,1)} %get-tuple-element.219.rest_0_.total_home), channel_id=1, source_target_pairs={{0,1},{3,2},{4,5},{7,6},{8,9},{11,10},{12,13},{15,14},{16,17},{19,... | collective-permute-start | bytes 4718600 | tf_op jit(solution)/shard_map/ppermute | solution.py:1207
  294.9 74.0 %collective-permute-start.22 = (bf16[512,1536]{1,0:T(8,128)(2,1)}, bf16[512,1536]{1,0:T(8,128)(2,1)}, u32[]{:S(2)}, u32[]{:S(2)}) collective-permute-start(bf16[512,1536]{1,0:T(8,128)(2,1)} %line_land.27.rest_0_.total_home), channel_id=1, source_target_pairs={{1,2},{2,1},{5,6},{6,5},{9,10},{10,9},{13,14},{14,13},{17,18},{18,... | collective-permute-start | bytes 4718600 | tf_op jit(solution)/shard_map/ppermute | solution.py:1207
  299.9 1.2 copy-start.9
  326.6 1.1 copy-start.14
  327.7 4.7 copy-start.7
  327.7 10.4 %copy-start = (bf16[512,1536]{1,0:T(8,128)(2,1)S(1)}, bf16[512,1536]{1,0:T(8,128)(2,1)}, u32[]{:S(2)}) copy-start(bf16[512,1536]{1,0:T(8,128)(2,1)} %line_land.28.rest_1_.total_home) | copy-start | bytes 4718596
  330.6 44.0 %collective-permute-start.25 = (bf16[512,1536]{1,0:T(8,128)(2,1)}, bf16[512,1536]{1,0:T(8,128)(2,1)}, u32[]{:S(2)}, u32[]{:S(2)}) collective-permute-start(bf16[512,1536]{1,0:T(8,128)(2,1)} %line_land.29.rest_7_.total_home), channel_id=1, source_target_pairs={{1,2},{2,1},{5,6},{6,5},{9,10},{10,9},{13,14},{14,13},{17,18},{18,... | collective-permute-start | bytes 4718600 | tf_op jit(solution)/shard_map/ppermute | solution.py:1207
  332.5 21.5 %collective-permute-start.19 = (bf16[256,1536]{1,0:T(8,128)(2,1)S(1)}, bf16[256,1536]{1,0:T(8,128)(2,1)S(1)}, u32[]{:S(2)}, u32[]{:S(2)}) collective-permute-start(bf16[256,1536]{1,0:T(8,128)(2,1)S(1)} %copy-done.7), channel_id=1, source_target_pairs={{0,1},{3,2},{4,5},{7,6},{8,9},{11,10},{12,13},{15,14},{16,17},{19,... | collective-permute-start | bytes 2359304 | tf_op jit(solution)/shard_map/ppermute | solution.py:1207
  335.9 30.8 %collective-permute-start.18 = (bf16[256,1536]{1,0:T(8,128)(2,1)}, bf16[256,1536]{1,0:T(8,128)(2,1)}, u32[]{:S(2)}, u32[]{:S(2)}) collective-permute-start(bf16[256,1536]{1,0:T(8,128)(2,1)} %get-tuple-element.228.total_home), channel_id=1, source_target_pairs={{0,1},{3,2},{4,5},{7,6},{8,9},{11,10},{12,13},{15,14},{16,17},{19,... | collective-permute-start | bytes 2359304 | tf_op jit(solution)/shard_map/ppermute | solution.py:1207
  338.1 42.2 %collective-permute-start.24 = (bf16[512,1536]{1,0:T(8,128)(2,1)S(1)}, bf16[512,1536]{1,0:T(8,128)(2,1)}, u32[]{:S(2)}, u32[]{:S(2)}) collective-permute-start(bf16[512,1536]{1,0:T(8,128)(2,1)S(1)} %copy-done), channel_id=1, source_target_pairs={{1,0},{2,3},{5,4},{6,7},{9,8},{10,11},{13,12},{14,15},{17,16},{18,... | collective-permute-start | bytes 4718600 | tf_op jit(solution)/shard_map/ppermute | solution.py:1207
  354.0 0.9 copy-start.17
  357.1 79.4 %all-reduce.5.cloned.1.call-start = ((), (), s32[]{:S(2)}) async-start(), calls=%async_computation | async-start | bytes 6488064 | tf_op jit(solution)/shard_map/psum | solution.py:1443
  368.9 4.2 copy-start.6
  371.8 40.0 %collective-permute-start.23 = (bf16[512,1536]{1,0:T(8,128)(2,1)}, bf16[512,1536]{1,0:T(8,128)(2,1)}, u32[]{:S(2)}, u32[]{:S(2)}) collective-permute-start(bf16[512,1536]{1,0:T(8,128)(2,1)} %line_land.32.rest_0_.total_home), channel_id=1, source_target_pairs={{1,0},{2,3},{5,4},{6,7},{9,8},{10,11},{13,12},{14,15},{17,16},{18,... | collective-permute-start | bytes 4718600 | tf_op jit(solution)/shard_map/ppermute | solution.py:1207
  373.1 11.0 %collective-permute-start.26 = (bf16[256,1536]{1,0:T(8,128)(2,1)S(1)}, bf16[256,1536]{1,0:T(8,128)(2,1)}, u32[]{:S(2)}, u32[]{:S(2)}) collective-permute-start(bf16[256,1536]{1,0:T(8,128)(2,1)S(1)} %copy-done.6), channel_id=1, source_target_pairs={{1,2},{2,1},{5,6},{6,5},{9,10},{10,9},{13,14},{14,13},{17,18},{18,... | collective-permute-start | bytes 2359304 | tf_op jit(solution)/shard_map/ppermute | solution.py:1207
  377.5 68.0 %collective-permute-start.29 = (bf16[512,1536]{1,0:T(8,128)(2,1)}, bf16[512,1536]{1,0:T(8,128)(2,1)}, u32[]{:S(2)}, u32[]{:S(2)}) collective-permute-start(bf16[512,1536]{1,0:T(8,128)(2,1)} %line_land.33.rest_0_.total_home), channel_id=1, source_target_pairs={{1,0},{2,3},{5,4},{6,7},{9,8},{10,11},{13,12},{14,15},{17,16},{18,... | collective-permute-start | bytes 4718600 | tf_op jit(solution)/shard_map/ppermute | solution.py:1207
  378.8 36.5 %collective-permute-start.21 = (bf16[256,1536]{1,0:T(8,128)(2,1)}, bf16[256,1536]{1,0:T(8,128)(2,1)}, u32[]{:S(2)}, u32[]{:S(2)}) collective-permute-start(bf16[256,1536]{1,0:T(8,128)(2,1)} %line_land.31.rest_0_.total_home), channel_id=1, source_target_pairs={{1,2},{2,1},{5,6},{6,5},{9,10},{10,9},{13,14},{14,13},{17,18},{18,... | collective-permute-start | bytes 2359304 | tf_op jit(solution)/shard_map/ppermute | solution.py:1207
  384.1 3.7 copy-start.5
  386.5 75.7 %collective-permute-start.28 = (bf16[256,1536]{1,0:T(8,128)(2,1)}, bf16[256,1536]{1,0:T(8,128)(2,1)S(1)}, u32[]{:S(2)}, u32[]{:S(2)}) collective-permute-start(bf16[256,1536]{1,0:T(8,128)(2,1)} %line_land.34.rest_1_.total_home), channel_id=1, source_target_pairs={{1,0},{2,3},{5,4},{6,7},{9,8},{10,11},{13,12},{14,15},{17,16},{18,... | collective-permute-start | bytes 2359304 | tf_op jit(solution)/shard_map/ppermute | solution.py:1207
  387.8 2.6 copy-start.4
  436.5 3.6 copy-start.18
  438.8 48.4 %collective-permute-start.27 = (bf16[256,1536]{1,0:T(8,128)(2,1)}, bf16[256,1536]{1,0:T(8,128)(2,1)S(1)}, u32[]{:S(2)}, u32[]{:S(2)}) collective-permute-start(bf16[256,1536]{1,0:T(8,128)(2,1)} %line_land.35.rest_1_.total_home), channel_id=1, source_target_pairs={{1,0},{2,3},{5,4},{6,7},{9,8},{10,11},{13,12},{14,15},{17,16},{18,... | collective-permute-start | bytes 2359304 | tf_op jit(solution)/shard_map/ppermute | solution.py:1207
  462.2 0.9 copy-start.16
  466.1 7.3 %copy-start.3 = (bf16[1536,768]{1,0:T(8,128)(2,1)S(1)}, bf16[1536,768]{1,0:T(8,128)(2,1)}, u32[]{:S(2)}) copy-start(bf16[1536,768]{1,0:T(8,128)(2,1)} %get-tuple-element.249.rest_1_) | copy-start | bytes 7077892
  468.4 22.7 %collective-permute-start.30 = (bf16[480,256]{1,0:T(8,128)(2,1)}, bf16[480,256]{1,0:T(8,128)(2,1)S(1)}, u32[]{:S(2)}, u32[]{:S(2)}) collective-permute-start(bf16[480,256]{1,0:T(8,128)(2,1)} %get-tuple-element.241), channel_id=1, source_target_pairs={{0,1},{1,0},{2,3},{3,2},{4,5},{5,4},{6,7},{7,6},{8,9},{9,8},{10,11... | collective-permute-start | bytes 737288 | tf_op jit(solution)/shard_map/ppermute | solution.py:1292
  468.4 22.8 %collective-permute-start.31 = (bf16[480,256]{1,0:T(8,128)(2,1)}, bf16[480,256]{1,0:T(8,128)(2,1)S(1)}, u32[]{:S(2)}, u32[]{:S(2)}) collective-permute-start(bf16[480,256]{1,0:T(8,128)(2,1)} %get-tuple-element.242), channel_id=1, source_target_pairs={{0,2},{1,3},{2,0},{3,1},{4,6},{5,7},{6,4},{7,5},{8,10},{9,11},{10,... | collective-permute-start | bytes 737288 | tf_op jit(solution)/shard_map/ppermute | solution.py:1292
  471.4 19.8 %collective-permute-start.32 = (bf16[480,256]{1,0:T(8,128)(2,1)}, bf16[480,256]{1,0:T(8,128)(2,1)S(1)}, u32[]{:S(2)}, u32[]{:S(2)}) collective-permute-start(bf16[480,256]{1,0:T(8,128)(2,1)} %get-tuple-element.243), channel_id=1, source_target_pairs={{0,3},{1,2},{2,1},{3,0},{4,7},{5,6},{6,5},{7,4},{8,11},{9,10},{10,... | collective-permute-start | bytes 737288 | tf_op jit(solution)/shard_map/ppermute | solution.py:1292
  487.2 0.9 copy-start.15
  491.1 0.7 copy-start.19
  491.2 0.8 copy-start.20
  491.2 0.9 copy-start.21
Sparse Core Ops, SparseCore 0:
  177.2 87.1 all-reduce.6
  362.5 73.9 all-reduce.4
